TPU v7x, 256 devices: a whole 4x4x8 slice. The times are simulated.
256 devices in a mesh: dp: 64 (over x, z, core), mp: 4 (over y).
Axes of the slice: x: 4, y: 4, z: 8, core: 2. Of those that a mesh axis runs over, the one named last changes fastest.
Arguments:
- big_q: bfloat16 [40960, 2560], P('dp', 'mp'), may hold values from -5 to 5
- big_k: bfloat16 [40960, 2560], P('dp', 'mp'), may hold values from -5 to 5
- big_v: bfloat16 [40960, 2560], P('dp', 'mp'), may hold values from -6 to 6
- big_dout: bfloat16 [40960, 2560], P('dp', 'mp'), may hold values from -6 to 6
- big_counts: int32 [64, 4], P('dp'), may hold values from 1 to 320, 640 in all within a row
- small_q: bfloat16 [32768, 2560], P('dp', 'mp'), may hold values from -5 to 5
- small_k: bfloat16 [32768, 2560], P('dp', 'mp'), may hold values from -5 to 5
- small_v: bfloat16 [32768, 2560], P('dp', 'mp'), may hold values from -6 to 6
- small_image: int32 [64, 512], replicated, may hold values from 0 to 47, never falling along the last dimension, each value on 1 to 16 neighbouring positions
- owner: int32 [3072, 1], replicated, may hold values from 0 to 63; in each aligned block of 48 rows (0 to 47, 48 to 95, ...) no two rows name the same one
- owner_dout: bfloat16 [65536, 2560], P('dp', 'mp'), may hold values from -6 to 6
- reward_w: float32 [2560], P('mp'), may hold values from -1.2 to 1.2
- pair_perm: int32 [3328], replicated, may hold values from 0 to 3327, each once
Outputs:
- big_out: bfloat16 [40960, 2560], P('dp', 'mp')
- small_out: bfloat16 [65536, 2560], P('dp', 'mp')
- big_dq: bfloat16 [40960, 2560], P('dp', 'mp')
- big_dk: bfloat16 [40960, 2560], P('dp', 'mp')
- big_dv: bfloat16 [40960, 2560], P('dp', 'mp')
- small_dq: bfloat16 [32768, 2560], P('dp', 'mp')
- small_dk: bfloat16 [32768, 2560], P('dp', 'mp')
- small_dv: bfloat16 [32768, 2560], P('dp', 'mp')
- pair_loss: float32 [1664], replicated
Inputs may be any that keep to these rules, and one draw needn't show every extreme that they name: `big_counts`: each row sums to 640; its largest entry is 320. `small_image`: numbers never fall along a row; every image of a row has 1 to 16 rows, and some image has exactly 16. At most 1 of the 48 small images of one device share an owner, and on some device exactly 1 do. `pair_perm`: each image number appears once.
All inputs are finite; a program needn't handle non-finite values.
Results may differ from a plain program's by a relative error of at most 0.03.
Values may be sent and summed in bfloat16 or wider, within the bound.
No kernel may reach another device: no remote copies, remote signals or barrier semaphores. Data moves between devices by JAX's collectives and lax.ppermute only.
A program may use at most 128 MiB of HBM per device.

v0:
```python
import math

import jax
import jax.numpy as jnp
from jax import lax
from jax.sharding import PartitionSpec as P

HD = 128
BIG_IMG = 4
MIG_IMG = 48
SMALL = 16


def probabilities(queries, key_rows, allowed):
    score_scale = 1.0 / math.sqrt(HD)
    raw_scores = (
        jnp.einsum("gqhd,gkhd->ghqk", queries, key_rows, preferred_element_type=jnp.float32)
        * score_scale
    )
    raw_scores = jnp.where(allowed[:, None], raw_scores, -1e30)
    row_max = jnp.max(raw_scores, axis=-1, keepdims=True)
    expon = jnp.exp(raw_scores - row_max)
    row_total = jnp.sum(expon, axis=-1, keepdims=True)
    return jnp.where(allowed[:, None], expon / row_total, 0.0).astype(jnp.bfloat16)


def attend(weights, values):
    return jnp.einsum(
        "ghqk,gkhd->gqhd", weights, values, preferred_element_type=jnp.float32
    ).astype(jnp.bfloat16)


def gradients(queries, key_rows, values, weights, cotangent):
    score_scale = 1.0 / math.sqrt(HD)
    prob_grad = jnp.einsum("gqhd,gkhd->ghqk", cotangent, values, preferred_element_type=jnp.float32)
    prob_rows = weights.astype(jnp.float32)
    row_dot = jnp.sum(prob_rows * prob_grad, axis=-1, keepdims=True)
    dscore = (prob_rows * (prob_grad - row_dot)).astype(jnp.bfloat16)
    value_grad = jnp.einsum(
        "ghqk,gqhd->gkhd", weights, cotangent, preferred_element_type=jnp.float32
    ).astype(jnp.bfloat16)
    query_grad = (
        jnp.einsum("ghqk,gkhd->gqhd", dscore, key_rows, preferred_element_type=jnp.float32)
        * score_scale
    ).astype(jnp.bfloat16)
    key_grad = (
        jnp.einsum("ghqk,gqhd->gkhd", dscore, queries, preferred_element_type=jnp.float32)
        * score_scale
    ).astype(jnp.bfloat16)
    return (query_grad, key_grad, value_grad)


def slot_tables(target, owners, slot_rank, small_count, slots):
    dev_count = owners.shape[0]
    positions = jnp.arange(slots, dtype=jnp.int32)
    images = jnp.arange(MIG_IMG, dtype=jnp.int32)
    chosen = (
        (owners[:, None, :] == target) & (slot_rank[:, None, :] == positions[None, :, None])
    ).astype(jnp.int32)
    length = jnp.sum(chosen * small_count[:, None, :], axis=2)
    global_id = (
        dev_count * BIG_IMG
        + jnp.arange(dev_count, dtype=jnp.int32)[:, None, None] * MIG_IMG
        + images
    )
    number = jnp.sum(chosen * global_id, axis=2)
    filled = jnp.sum(chosen, axis=2)
    return (length, number, filled)


def on_device(
    big_q,
    big_k,
    big_v,
    big_dout,
    big_counts,
    small_q,
    small_k,
    small_v,
    small_image,
    owner,
    owner_dout,
    reward_w,
    pair_perm,
):
    dev_count = lax.axis_size("dp")
    device_index = lax.axis_index("dp")
    features = big_q.shape[1]
    head_count = features // HD
    big_rows = big_q.shape[0]
    small_rows = small_q.shape[0]
    slots = (MIG_IMG + dev_count - 1) // dev_count
    slot_rows = slots * SMALL

    def grouped(source_rows, group_rows):
        return source_rows.reshape(-1, group_rows, head_count, HD)

    counts = big_counts[0]
    big_ends = jnp.cumsum(counts)
    starts = big_ends - counts
    row_index = jnp.arange(big_rows, dtype=jnp.int32)
    big_seg = jnp.sum((row_index[:, None] >= big_ends[None, :]).astype(jnp.int32), axis=1)
    big_class = jnp.any(row_index[:, None] == starts[None, :], axis=1)
    big_allowed = (big_seg[:, None] == big_seg[None, :])[None]
    big_weights = probabilities(grouped(big_q, big_rows), grouped(big_k, big_rows), big_allowed)
    big_out = attend(big_weights, grouped(big_v, big_rows)).reshape(big_rows, features)
    images = jnp.arange(MIG_IMG, dtype=jnp.int32)
    slot_steps = jnp.arange(SMALL, dtype=jnp.int32)
    owners = owner.reshape(dev_count, MIG_IMG)
    small_count = jnp.sum((small_image[:, :, None] == images).astype(jnp.int32), axis=1)
    small_start = jnp.cumsum(small_count, axis=1) - small_count
    before = images[None, :] < images[:, None]
    slot_rank = jnp.sum(
        ((owners[:, :, None] == owners[:, None, :]) & before[None]).astype(jnp.int32), axis=2
    )
    my_count = lax.dynamic_slice_in_dim(small_count, device_index, 1, 0)[0]
    my_start = lax.dynamic_slice_in_dim(small_start, device_index, 1, 0)[0]
    my_owner = lax.dynamic_slice_in_dim(owners, device_index, 1, 0)[0]
    my_rank = lax.dynamic_slice_in_dim(slot_rank, device_index, 1, 0)[0]
    is_live = slot_steps[None, :] < my_count[:, None]
    source = my_start[:, None] + slot_steps
    gather_at = jnp.where(is_live, source, 0).reshape(-1)
    scatter_at = jnp.where(is_live, source, small_rows).reshape(-1)
    slot_dest = ((my_owner * slot_rows + my_rank * SMALL)[:, None] + slot_steps).reshape(-1)
    live_flat = is_live.reshape(-1)

    def padded(source_rows):
        return jnp.where(live_flat[:, None], source_rows[gather_at], 0)

    def to_rows(padded_grad):
        blank_rows = jnp.zeros((small_rows, features), jnp.bfloat16)
        return blank_rows.at[scatter_at].set(padded_grad, mode="drop")

    pad_queries = padded(small_q)
    pad_keys = padded(small_k)
    pad_values = padded(small_v)
    blank_slots = jnp.zeros((dev_count * slot_rows, features), jnp.bfloat16)
    big_ids = device_index * BIG_IMG + jnp.arange(BIG_IMG, dtype=jnp.int32)
    big_part = jnp.sum(big_out[starts].astype(jnp.float32) * reward_w, axis=1)
    out_queries = blank_slots.at[slot_dest].set(pad_queries)
    out_keys = blank_slots.at[slot_dest].set(pad_keys)
    out_values = blank_slots.at[slot_dest].set(pad_values)
    work_queries, work_keys, work_values = (
        lax.all_to_all(out_queries, "dp", split_axis=0, concat_axis=0, tiled=True),
        lax.all_to_all(out_keys, "dp", split_axis=0, concat_axis=0, tiled=True),
        lax.all_to_all(out_values, "dp", split_axis=0, concat_axis=0, tiled=True),
    )
    slot_len, slot_id, slot_fill = slot_tables(device_index, owners, slot_rank, small_count, slots)
    slot_live = slot_steps[None, :] < slot_len.reshape(-1)[:, None]
    small_allowed = slot_live[:, :, None] & slot_live[:, None, :]
    small_weights = probabilities(
        grouped(work_queries, SMALL), grouped(work_keys, SMALL), small_allowed
    )
    small_rows_out = attend(small_weights, grouped(work_values, SMALL))
    small_out = small_rows_out.reshape(dev_count * slot_rows, features)
    small_ids = slot_id.reshape(-1)
    small_part = jnp.sum(
        small_rows_out[:, 0].reshape(-1, features).astype(jnp.float32) * reward_w, axis=1
    )
    image_total = dev_count * (BIG_IMG + MIG_IMG)
    partial_scores = (
        jnp.zeros((image_total,), jnp.float32)
        .at[big_ids]
        .add(big_part)
        .at[small_ids]
        .add(small_part)
    )
    scores = lax.psum(partial_scores, ("dp", "mp"))
    preferred = pair_perm[0::2]
    rejected = pair_perm[1::2]
    margin = scores[rejected] - scores[preferred]
    pair_loss = jax.nn.softplus(margin)
    pull_back = jax.nn.sigmoid(margin)
    image_gain = (
        jnp.zeros((image_total,), jnp.float32)
        .at[preferred]
        .set(-pull_back)
        .at[rejected]
        .set(pull_back)
    )
    big_gain = lax.dynamic_slice_in_dim(image_gain, device_index * BIG_IMG, BIG_IMG)
    big_hot = big_seg[:, None] == jnp.arange(BIG_IMG, dtype=jnp.int32)
    row_gain = jnp.sum(jnp.where(big_hot, big_gain[None, :], 0.0), axis=1) * big_class.astype(
        jnp.float32
    )
    big_cot = (big_dout.astype(jnp.float32) + row_gain[:, None] * reward_w).astype(jnp.bfloat16)
    big_dq, big_dk, big_dv = gradients(
        grouped(big_q, big_rows),
        grouped(big_k, big_rows),
        grouped(big_v, big_rows),
        big_weights,
        grouped(big_cot, big_rows),
    )
    first_row = (slot_steps == 0).astype(jnp.float32)
    slot_gain = image_gain[slot_id.reshape(-1)] * slot_fill.reshape(-1).astype(jnp.float32)
    cotangent = owner_dout.reshape(-1, SMALL, features).astype(jnp.float32)
    cotangent = cotangent + slot_gain[:, None, None] * first_row[None, :, None] * reward_w
    query_grad, key_grad, value_grad = gradients(
        grouped(work_queries, SMALL),
        grouped(work_keys, SMALL),
        grouped(work_values, SMALL),
        small_weights,
        grouped(cotangent.astype(jnp.bfloat16), SMALL),
    )
    back_queries, back_keys, back_values = (
        lax.all_to_all(
            query_grad.reshape(-1, features), "dp", split_axis=0, concat_axis=0, tiled=True
        ),
        lax.all_to_all(
            key_grad.reshape(-1, features), "dp", split_axis=0, concat_axis=0, tiled=True
        ),
        lax.all_to_all(
            value_grad.reshape(-1, features), "dp", split_axis=0, concat_axis=0, tiled=True
        ),
    )
    small_dq = to_rows(back_queries[slot_dest])
    small_dk = to_rows(back_keys[slot_dest])
    small_dv = to_rows(back_values[slot_dest])
    return (
        big_out,
        small_out,
        big_dq.reshape(big_rows, features),
        big_dk.reshape(big_rows, features),
        big_dv.reshape(big_rows, features),
        small_dq,
        small_dk,
        small_dv,
        pair_loss,
    )


def solution(mesh):
    placed = (
        P("dp", "mp"),
        P("dp", "mp"),
        P("dp", "mp"),
        P("dp", "mp"),
        P("dp", None),
        P("dp", "mp"),
        P("dp", "mp"),
        P("dp", "mp"),
        P(),
        P(),
        P("dp", "mp"),
        P("mp"),
        P(),
    )
    return jax.shard_map(
        on_device,
        mesh=mesh,
        in_specs=placed,
        out_specs=(
            P("dp", "mp"),
            P("dp", "mp"),
            P("dp", "mp"),
            P("dp", "mp"),
            P("dp", "mp"),
            P("dp", "mp"),
            P("dp", "mp"),
            P("dp", "mp"),
            P(),
        ),
        check_vma=False,
    )
```

profile of v0, /device:TPU:1, one launch (start us, length us, event | category | flops | bytes accessed | tf_op | source)
XLA Modules:
  0.0 449.7 jit_solution(12866738618569935713)
XLA Ops:
  6.9 12.6 %scatter_custom_fusion.1 = bf16[1024,640]{1,0:T(8,128)(2,1)} fusion(s32[768]{0:T(1024)S(1)} %fusion.69, pred[768]{0:T(1024)(128)(4,1)S(1)} %lt.166, bf16[]{:T(256)} %constant.24.clone.1, bf16[512,640]{1,0:T(8,128)(2,1)S(1)} %copy-done, s32[1024]{0:T(1024)S(1)} %pad_clamp_fusion.5), kind=kCustom, calls=%fused_computation.87 | custom fusion | flops 491520 | bytes 1972224 | tf_op jit(solution)/shard_map/scatter | solution.py:140
  19.6 13.9 %all-to-all-start.1 = ((bf16[64,16,640]{2,1,0:T(8,128)(2,1)}), bf16[64,16,640]{2,1,0:T(8,128)(2,1)}, u32[]{:S(2)}, u32[]{:S(2)}) async-start(bf16[64,16,640]{2,1,0:T(8,128)(2,1)} %bitcast.12), calls=%async_computation.1 | async-start | bytes 2621440 | tf_op jit(solution)/shard_map/all_to_all | solution.py:144
  34.3 12.8 %scatter_custom_fusion.2 = bf16[1024,640]{1,0:T(8,128)(2,1)} fusion(s32[768]{0:T(1024)S(1)} %fusion.69, pred[768]{0:T(1024)(128)(4,1)S(1)} %lt.166, bf16[]{:T(256)} %constant.24.clone.1, bf16[512,640]{1,0:T(8,128)(2,1)S(1)} %copy-done.20, s32[1024]{0:T(1024)S(1)} %pad_clamp_fusion.5), kind=kCustom, calls=%fused_computation.85 | custom fusion | flops 491520 | bytes 1972224 | tf_op jit(solution)/shard_map/scatter | solution.py:141
  47.4 12.6 %scatter_custom_fusion = bf16[1024,640]{1,0:T(8,128)(2,1)} fusion(s32[768]{0:T(1024)S(1)} %fusion.69, pred[768]{0:T(1024)(128)(4,1)S(1)} %lt.166, bf16[]{:T(256)} %constant.24.clone.1, bf16[512,640]{1,0:T(8,128)(2,1)S(1)} %copy-done.21, s32[1024]{0:T(1024)S(1)} %pad_clamp_fusion.5), kind=kCustom, calls=%fused_computation.89 | custom fusion | flops 491520 | bytes 1972224 | tf_op jit(solution)/shard_map/scatter | solution.py:142
  65.0 2.4 all-to-all-done.1
  67.4 8.6 %all-to-all-start.2 = ((bf16[64,16,640]{2,1,0:T(8,128)(2,1)}), bf16[64,16,640]{2,1,0:T(8,128)(2,1)}, u32[]{:S(2)}, u32[]{:S(2)}) async-start(bf16[64,16,640]{2,1,0:T(8,128)(2,1)} %bitcast.167), calls=%async_computation.2 | async-start | bytes 2621440 | tf_op jit(solution)/shard_map/all_to_all | solution.py:145
  76.0 6.1 %fusion.87 = (f32[5,640]{1,0:T(8,128)S(1)}, f32[5,640,640]{1,2,0:T(8,128)}) fusion(pred[640,640]{0,1:T(8,128)(4,1)S(1)} %broadcast_compare_fusion, bf16[640,5,128]{0,2,1:T(8,128)(2,1)S(1)} %bitcast.171, bf16[640,5,128]{0,2,1:T(8,128)(2,1)S(1)} %bitcast.161), kind=kOutput, calls=%fused_computation.178 | convolution fusion | flops 532480640 | bytes 10252800 | tf_op jit(solution)/shard_map/sub | solution.py:22
  82.1 4.2 select_convert_fusion
  89.3 4.6 %reshape.632 = f32[64,16,5,128]{3,2,1,0:T(8,128)} reshape(bf16[1024,640]{1,0:T(8,128)(2,1)} %param.23) | data formatting | bytes 3932160 | tf_op jit(solution)/shard_map/convert_element_type | solution.py:196
  95.2 14.7 %all-to-all-done.2 = bf16[64,16,640]{2,1,0:T(8,128)(2,1)} async-done(((bf16[64,16,640]{2,1,0:T(8,128)(2,1)}), bf16[64,16,640]{2,1,0:T(8,128)(2,1)}, u32[]{:S(2)}, u32[]{:S(2)}) %all-to-all-start.2) | async-done | bytes 1310752 | tf_op jit(solution)/shard_map/all_to_all | solution.py:145
  109.9 6.2 %all-to-all-start = ((bf16[64,16,640]{2,1,0:T(8,128)(2,1)}), bf16[64,16,640]{2,1,0:T(8,128)(2,1)S(1)}, u32[]{:S(2)}, u32[]{:S(2)}) async-start(bf16[64,16,640]{2,1,0:T(8,128)(2,1)} %bitcast.11), calls=%async_computation | async-start | bytes 2621440 | tf_op jit(solution)/shard_map/all_to_all | solution.py:146
  116.6 4.6 %fusion.88 = (f32[64,5,16]{2,1,0:T(8,128)S(1)}, f32[64,5,16,16]{2,3,1,0:T(8,128)}) fusion(pred[64,16,16]{1,2,0:T(8,128)(4,1)S(1)} %broadcast_and_fusion, bf16[64,16,640]{2,1,0:T(8,128)(2,1)} %all-to-all-done.2, bf16[64,16,640]{2,1,0:T(8,128)(2,1)} %all-to-all-done.1), kind=kOutput, calls=%fused_computation.179 | convolution fusion | flops 21299216 | bytes 2985984 | tf_op jit(solution)/shard_map/sub | solution.py:22
  121.2 2.2 select_convert_fusion.1
  123.4 26.9 %all-to-all-done = bf16[64,16,640]{2,1,0:T(8,128)(2,1)S(1)} async-done(((bf16[64,16,640]{2,1,0:T(8,128)(2,1)}), bf16[64,16,640]{2,1,0:T(8,128)(2,1)S(1)}, u32[]{:S(2)}, u32[]{:S(2)}) %all-to-all-start) | async-done | bytes 1310752 | tf_op jit(solution)/shard_map/all_to_all | solution.py:146
  153.5 76.6 %psum.7 = f32[3328]{0:T(1024)S(1)} all-reduce(f32[3328]{0:T(1024)S(1)} %scatter_fusion), channel_id=1, replica_groups=mesh['dp'=64,'mp'=4] {'dp','mp'}, use_global_device_ids=true, to_apply=%region_19.20 | all-reduce | flops 3328 | bytes 26624 | tf_op jit(solution)/shard_map/psum | solution.py:168
  230.1 9.1 %gather_fusion.1 = f32[1664]{0:T(1024)S(1)} fusion(f32[3328]{0:T(1024)S(1)} %psum.7, s32[2048]{0:T(1024)S(1)} %pad_clamp_fusion.1), kind=kCustom, calls=%fused_computation.4 | custom fusion | bytes 19968 | tf_op jit(solution)/shard_map/gather | solution.py:171
  239.2 9.1 %gather_fusion.2 = f32[1664]{0:T(1024)S(1)} fusion(f32[3328]{0:T(1024)S(1)} %psum.7, s32[2048]{0:T(1024)S(1)} %pad_clamp_fusion), kind=kCustom, calls=%fused_computation.5 | custom fusion | bytes 19968 | tf_op jit(solution)/shard_map/gather | solution.py:171
  248.9 8.8 %scatter_custom_fusion.5 = f32[3328]{0:T(1024)S(1)} fusion(s32[1664]{0:T(1024)S(1)} %compare_select_fusion.2, f32[1664]{0:T(1024)S(1)} %get-tuple-element.47, f32[]{:T(128)} %constant.23.clone.1), kind=kCustom, calls=%fused_computation.142 | custom fusion | bytes 13316 | tf_op jit(solution)/shard_map/scatter | solution.py:177
  257.7 8.8 %scatter_fusion.1 = f32[3328]{0:T(1024)S(1)} fusion(f32[3328]{0:T(1024)S(1)} %scatter_custom_fusion.5, s32[1664]{0:T(1024)S(1)} %compare_select_fusion.1, f32[1664]{0:T(1024)S(1)} %get-tuple-element.48), kind=kCustom, calls=%fused_computation.16 | custom fusion | bytes 26624 | tf_op jit(solution)/shard_map/scatter | solution.py:179
  267.4 2.9 add_convert_fusion
  277.2 6.0 %all-to-all-start.4 = ((bf16[64,16,640]{2,1,0:T(8,128)(2,1)}), bf16[64,16,640]{2,1,0:T(8,128)(2,1)}, u32[]{:S(2)}, u32[]{:S(2)}) async-start(bf16[64,16,640]{2,1,0:T(8,128)(2,1)} %bitcast.168), calls=%async_computation.4 | async-start | bytes 2621440 | tf_op jit(solution)/shard_map/all_to_all | solution.py:209
  286.4 30.9 %all-to-all-done.4 = bf16[64,16,640]{2,1,0:T(8,128)(2,1)} async-done(((bf16[64,16,640]{2,1,0:T(8,128)(2,1)}), bf16[64,16,640]{2,1,0:T(8,128)(2,1)}, u32[]{:S(2)}, u32[]{:S(2)}) %all-to-all-start.4) | async-done | bytes 1310752 | tf_op jit(solution)/shard_map/all_to_all | solution.py:209
  317.2 6.5 %all-to-all-start.3 = ((bf16[64,16,640]{2,1,0:T(8,128)(2,1)}), bf16[64,16,640]{2,1,0:T(8,128)(2,1)}, u32[]{:S(2)}, u32[]{:S(2)}) async-start(bf16[64,16,640]{2,1,0:T(8,128)(2,1)} %bitcast.166), calls=%async_computation.3 | async-start | bytes 2621440 | tf_op jit(solution)/shard_map/all_to_all | solution.py:206
  323.8 2.2 copy.126
  334.2 23.6 %all-to-all-done.3 = bf16[64,16,640]{2,1,0:T(8,128)(2,1)} async-done(((bf16[64,16,640]{2,1,0:T(8,128)(2,1)}), bf16[64,16,640]{2,1,0:T(8,128)(2,1)}, u32[]{:S(2)}, u32[]{:S(2)}) %all-to-all-start.3) | async-done | bytes 1310752 | tf_op jit(solution)/shard_map/all_to_all | solution.py:206
  357.8 6.7 %all-to-all-start.5 = ((bf16[64,16,640]{2,1,0:T(8,128)(2,1)}), bf16[64,16,640]{2,1,0:T(8,128)(2,1)}, u32[]{:S(2)}, u32[]{:S(2)}) async-start(bf16[64,16,640]{2,1,0:T(8,128)(2,1)} %bitcast.165), calls=%async_computation.5 | async-start | bytes 2621440 | tf_op jit(solution)/shard_map/all_to_all | solution.py:212
  364.5 3.5 fusion.2
  368.0 4.4 fusion.3
  375.6 4.4 multiply_convert_fusion.3
  383.5 22.1 %scatter_custom_fusion.8 = bf16[512,640]{1,0:T(8,128)(2,1)} fusion(s32[768]{0:T(1024)S(1)} %fusion.71, bf16[1024,640]{1,0:T(8,128)(2,1)} %bitcast.41, s32[1024]{0:T(1024)S(1)} %pad_clamp_fusion.2, bf16[]{:T(256)} %constant.24.clone.1), kind=kCustom, calls=%fused_computation.81 | custom fusion | bytes 655872 | tf_op jit(solution)/shard_map/scatter | solution.py:132
  405.6 21.9 %scatter_custom_fusion.7 = bf16[512,640]{1,0:T(8,128)(2,1)} fusion(s32[768]{0:T(1024)S(1)} %fusion.71, bf16[1024,640]{1,0:T(8,128)(2,1)} %bitcast.39, s32[1024]{0:T(1024)S(1)} %pad_clamp_fusion.2, bf16[]{:T(256)} %constant.24.clone.1), kind=kCustom, calls=%fused_computation.83 | custom fusion | bytes 655872 | tf_op jit(solution)/shard_map/scatter | solution.py:132
  427.5 21.9 %scatter_custom_fusion.9 = bf16[512,640]{1,0:T(8,128)(2,1)} fusion(s32[768]{0:T(1024)S(1)} %fusion.71, bf16[1024,640]{1,0:T(8,128)(2,1)} %bitcast.43, s32[1024]{0:T(1024)S(1)} %pad_clamp_fusion.2, bf16[]{:T(256)} %constant.24.clone.1), kind=kCustom, calls=%fused_computation.79 | custom fusion | bytes 655872 | tf_op jit(solution)/shard_map/scatter | solution.py:132
  (137 shorter events, 46.4 us)
Async XLA Ops:
  0.6 6.3 %copy-start = (bf16[512,640]{1,0:T(8,128)(2,1)S(1)}, bf16[512,640]{1,0:T(8,128)(2,1)}, u32[]{:S(2)}) copy-start(bf16[512,640]{1,0:T(8,128)(2,1)} %param.18) | copy-start | bytes 1966084
  19.6 14.0 %copy-start.25 = (s32[3328]{0:T(1024)S(1)}, s32[3328]{0:T(1024)}, u32[]{:S(2)}) copy-start(s32[3328]{0:T(1024)} %param.25) | copy-start | bytes 39940
  19.6 14.7 %copy-start.20 = (bf16[512,640]{1,0:T(8,128)(2,1)S(1)}, bf16[512,640]{1,0:T(8,128)(2,1)}, u32[]{:S(2)}) copy-start(bf16[512,640]{1,0:T(8,128)(2,1)} %param.19) | copy-start | bytes 1966084
  19.6 47.9 %all-to-all-start.1 = ((bf16[64,16,640]{2,1,0:T(8,128)(2,1)}), bf16[64,16,640]{2,1,0:T(8,128)(2,1)}, u32[]{:S(2)}, u32[]{:S(2)}) async-start(bf16[64,16,640]{2,1,0:T(8,128)(2,1)} %bitcast.12), calls=%async_computation.1 | async-start | bytes 2621440 | tf_op jit(solution)/shard_map/all_to_all | solution.py:144
  33.5 13.6 %copy-start.24 = (s32[3072,1]{0,1:T(1,128)S(1)}, s32[3072,1]{0,1:T(1,128)}, u32[]{:S(2)}) copy-start(s32[3072,1]{0,1:T(1,128)} %param.22) | copy-start | bytes 36868
  33.5 13.8 %copy-start.21 = (bf16[512,640]{1,0:T(8,128)(2,1)S(1)}, bf16[512,640]{1,0:T(8,128)(2,1)}, u32[]{:S(2)}) copy-start(bf16[512,640]{1,0:T(8,128)(2,1)} %param.20) | copy-start | bytes 1966084
  34.3 25.7 %copy-start.26 = (s32[1,4]{1,0:T(1,128)S(1)}, s32[1,4]{1,0:T(1,128)}, u32[]{:S(2)}) copy-start(s32[1,4]{1,0:T(1,128)} %param.17) | copy-start | bytes 52
  34.3 25.9 %copy-start.16 = (bf16[640,640]{1,0:T(8,128)(2,1)S(1)}, bf16[640,640]{1,0:T(8,128)(2,1)}, u32[]{:S(2)}) copy-start(bf16[640,640]{1,0:T(8,128)(2,1)} %param.13) | copy-start | bytes 2457604
  47.4 14.1 %copy-start.17 = (bf16[640,640]{1,0:T(8,128)(2,1)S(1)}, bf16[640,640]{1,0:T(8,128)(2,1)}, u32[]{:S(2)}) copy-start(bf16[640,640]{1,0:T(8,128)(2,1)} %param.14) | copy-start | bytes 2457604
  62.4 13.6 %copy-start.13 = (bf16[640,640]{0,1:T(8,128)(2,1)}, bf16[640,640]{0,1:T(8,128)(2,1)S(1)}, u32[]{:S(2)}) copy-start(bf16[640,640]{0,1:T(8,128)(2,1)S(1)} %copy.111) | copy-start | bytes 2457604
  64.6 21.8 %copy-start.5 = (bf16[640,640]{0,1:T(8,128)(2,1)}, bf16[640,640]{0,1:T(8,128)(2,1)S(1)}, u32[]{:S(2)}) copy-start(bf16[640,640]{0,1:T(8,128)(2,1)S(1)} %copy.114) | copy-start | bytes 2457604
  64.6 11.5 %copy-start.18 = (bf16[640,640]{0,1:T(8,128)(2,1)S(1)}, bf16[640,640]{0,1:T(8,128)(2,1)}, u32[]{:S(2)}) copy-start(bf16[640,640]{0,1:T(8,128)(2,1)} %copy.110) | copy-start | bytes 2457604
  67.4 42.5 %all-to-all-start.2 = ((bf16[64,16,640]{2,1,0:T(8,128)(2,1)}), bf16[64,16,640]{2,1,0:T(8,128)(2,1)}, u32[]{:S(2)}, u32[]{:S(2)}) async-start(bf16[64,16,640]{2,1,0:T(8,128)(2,1)} %bitcast.167), calls=%async_computation.2 | async-start | bytes 2621440 | tf_op jit(solution)/shard_map/all_to_all | solution.py:145
  86.4 1.9 copy-start.2
  89.2 4.6 %copy-start.15 = (bf16[640,640]{1,0:T(8,128)(2,1)}, bf16[640,640]{1,0:T(8,128)(2,1)S(1)}, u32[]{:S(2)}) copy-start(bf16[640,640]{1,0:T(8,128)(2,1)S(1)} %copy.143) | copy-start | bytes 2457604
  89.2 5.2 %copy-start.23 = (f32[640]{0:T(1024)S(1)}, f32[640]{0:T(1024)}, u32[]{:S(2)}) copy-start(f32[640]{0:T(1024)} %param.24) | copy-start | bytes 7684
  109.9 40.4 %all-to-all-start = ((bf16[64,16,640]{2,1,0:T(8,128)(2,1)}), bf16[64,16,640]{2,1,0:T(8,128)(2,1)S(1)}, u32[]{:S(2)}, u32[]{:S(2)}) async-start(bf16[64,16,640]{2,1,0:T(8,128)(2,1)} %bitcast.11), calls=%async_computation | async-start | bytes 2621440 | tf_op jit(solution)/shard_map/all_to_all | solution.py:146
  270.3 1.3 copy-start.7
  270.3 2.5 copy-start.9
  277.2 40.1 %all-to-all-start.4 = ((bf16[64,16,640]{2,1,0:T(8,128)(2,1)}), bf16[64,16,640]{2,1,0:T(8,128)(2,1)}, u32[]{:S(2)}, u32[]{:S(2)}) async-start(bf16[64,16,640]{2,1,0:T(8,128)(2,1)} %bitcast.168), calls=%async_computation.4 | async-start | bytes 2621440 | tf_op jit(solution)/shard_map/all_to_all | solution.py:209
  286.4 37.4 %copy-start.22 = (s32[48,16]{1,0:T(8,128)S(1)}, s32[48,16]{1,0:T(8,128)}, u32[]{:S(2)}) copy-start(s32[48,16]{1,0:T(8,128)} %get-tuple-element.53) | copy-start | bytes 9220
  317.2 8.9 %copy-start.12 = (bf16[64,16,5,128]{3,1,2,0:T(8,128)(2,1)S(1)}, bf16[64,16,5,128]{3,1,2,0:T(8,128)(2,1)}, u32[]{:S(2)}) copy-start(bf16[64,16,5,128]{3,1,2,0:T(8,128)(2,1)} %copy-done.11) | copy-start | bytes 3932164
  317.2 40.6 %all-to-all-start.3 = ((bf16[64,16,640]{2,1,0:T(8,128)(2,1)}), bf16[64,16,640]{2,1,0:T(8,128)(2,1)}, u32[]{:S(2)}, u32[]{:S(2)}) async-start(bf16[64,16,640]{2,1,0:T(8,128)(2,1)} %bitcast.166), calls=%async_computation.3 | async-start | bytes 2621440 | tf_op jit(solution)/shard_map/all_to_all | solution.py:206
  326.1 2.0 copy-start.8
  328.1 2.3 copy-start.14
  328.9 2.7 copy-start.3
  334.2 30.3 %copy-start.6 = (bf16[640,640]{0,1:T(8,128)(2,1)S(1)}, bf16[640,640]{0,1:T(8,128)(2,1)}, u32[]{:S(2)}) copy-start(bf16[640,640]{0,1:T(8,128)(2,1)} %copy-done.5) | copy-start | bytes 2457604
  357.8 69.7 %all-to-all-start.5 = ((bf16[64,16,640]{2,1,0:T(8,128)(2,1)}), bf16[64,16,640]{2,1,0:T(8,128)(2,1)}, u32[]{:S(2)}, u32[]{:S(2)}) async-start(bf16[64,16,640]{2,1,0:T(8,128)(2,1)} %bitcast.165), calls=%async_computation.5 | async-start | bytes 2621440 | tf_op jit(solution)/shard_map/all_to_all | solution.py:212
  368.0 4.4 copy-start.19
  372.4 1.9 copy-start.4
  375.6 6.6 %copy-start.10 = (bf16[64,16,5,128]{3,2,1,0:T(8,128)(2,1)S(1)}, bf16[64,16,5,128]{3,2,1,0:T(8,128)(2,1)}, u32[]{:S(2)}) copy-start(bf16[64,16,5,128]{3,2,1,0:T(8,128)(2,1)} %copy.125) | copy-start | bytes 3932164
  382.1 67.3 %copy-start.1 = (bf16[512,640]{1,0:T(8,128)(2,1)S(1)}, bf16[512,640]{1,0:T(8,128)(2,1)}, u32[]{:S(2)}) copy-start(bf16[512,640]{1,0:T(8,128)(2,1)} %param.18) | copy-start | bytes 1966084
  (1 other events, 1.1 us)
where the time goes:
time: 458 us; the launch traced here: 450 us
  local copies, waits for them, and re-layouts  134 us (29%)
  waiting for transfers between devices  98.6 us (22%)
  blocking collectives  76.6 us (17%)
  other arithmetic  62.4 us (14%)
  starting transfers between devices  47.8 us (10%)
  matrix products  28.4 us (6%)
    psum x1, blocking collectives, on_device(): scores = lax.psum(partial_scores, ('dp', 'mp'))  76.6 us
    scatter x3, local copies, waits for them, and re-layouts, to_rows(): return blank_rows.at[scatter_at].set(padded_grad, mode='drop')  66 us
    all_to_all x1, waiting for transfers between devices, on_device(): lax.all_to_all(key_grad.reshape(-1, features), 'dp', split_axis=0, concat...  30.9 us
    all_to_all x1, waiting for transfers between devices, on_device(): lax.all_to_all(out_values, 'dp', split_axis=0, concat_axis=0, tiled=True)  26.9 us
    all_to_all x1, waiting for transfers between devices, on_device(): lax.all_to_all(query_grad.reshape(-1, features), 'dp', split_axis=0, conc...  23.6 us
    unnamed x64, local copies, waits for them, and re-layouts  19.3 us
    gather x2, local copies, waits for them, and re-layouts, on_device(): margin = scores[rejected] - scores[preferred]  18.2 us
    scatter x2, local copies, waits for them, and re-layouts, on_device(): image_gain = jnp.zeros((image_total,), jnp.float32).at[preferred].set(-pu...  17.6 us
  transfers between devices with their start and end apart: 6, of which 5 were waited for; matrix products, arithmetic and copies ran while one was open for 29% of the time, Pallas kernels for 0%

commit v1 on v0

v1 whole, which is shorter than its diff:
```python
import functools
import math

import jax
import jax.numpy as jnp
from jax import lax
from jax.experimental import pallas as pl
from jax.experimental.pallas import tpu as pltpu
from jax.sharding import PartitionSpec as P

HD = 128
BIG_IMG = 4
MIG_IMG = 48
SMALL = 16
LANES = 128
IMAGES = BIG_IMG + MIG_IMG
SCALE = 1.0 / math.sqrt(HD)
EXP2_SCALE = SCALE * math.log2(math.e)
BLOCK = 128
WINDOW = 256
MASKED = -1e30


def mm(left, right):
    return jnp.dot(left, right, preferred_element_type=jnp.float32)


def mm_nt(left, right):
    return lax.dot_general(
        left, right, (((1,), (1,)), ((), ())), preferred_element_type=jnp.float32
    )


def mm_tn(left, right):
    return lax.dot_general(
        left, right, (((0,), (0,)), ((), ())), preferred_element_type=jnp.float32
    )


def iota(shape, dim):
    return lax.broadcasted_iota(jnp.int32, shape, dim)


def windows(rows):
    pairs = []
    for start in range(0, rows, BLOCK):
        pairs.append((start, min(max(start - (WINDOW - BLOCK) // 2, 0), rows - WINDOW)))
    return pairs


def image_ends(counts):
    first = counts[0]
    second = first + counts[1]
    third = second + counts[2]
    return first, second, third


def segment_of(rows, ends):
    return sum((rows >= end).astype(jnp.int32) for end in ends)


def class_mask_big(rows, counts):
    ends = image_ends(counts)
    lane = iota((rows, LANES), 1)
    start = jnp.where(
        lane == 0,
        0,
        jnp.where(
            lane == 1,
            ends[0],
            jnp.where(lane == 2, ends[1], jnp.where(lane == 3, ends[2], -1)),
        ),
    )
    return (iota((rows, LANES), 0) == start).astype(jnp.float32)


def small_tables(dev, image_ref, owner_ref):
    image = image_ref[pl.ds(lax.rem(dev, 8), 1), :]
    rows = image.shape[1]
    image_f = image.astype(jnp.float32)
    spread = jnp.broadcast_to(image_f, (LANES, rows))
    image_col = jnp.transpose(spread)
    before = jnp.zeros((1, rows), jnp.float32)
    for start in range(0, rows, LANES):
        column = image_col[start : start + LANES, 0:1]
        before = before + jnp.sum(
            (column < image_f).astype(jnp.float32), axis=0, keepdims=True
        )
    position = iota((1, rows), 1).astype(jnp.float32) - before
    owners = owner_ref[...].astype(jnp.float32)
    hot = iota((MIG_IMG, rows), 0) == image
    owner_row = jnp.sum(jnp.where(hot, owners, 0.0), axis=0, keepdims=True)
    dest = owner_row * SMALL + position
    sub = iota((LANES, rows), 0)
    stacked = jnp.where(sub == 0, image_f, jnp.where(sub == 1, position, dest))
    columns = jnp.transpose(stacked)
    return image, dest.astype(jnp.int32), columns


def class_mask_small(columns):
    lane = iota(columns.shape, 1)
    image = columns[:, 0:1].astype(jnp.int32)
    first = columns[:, 1:2] == 0.0
    return ((image + BIG_IMG == lane) & first).astype(jnp.float32)


def probs(queries, keys, allowed):
    scores = jnp.where(allowed, mm_nt(queries, keys), MASKED)
    top = jnp.max(scores, axis=-1, keepdims=True)
    grown = jnp.exp2((scores - top) * EXP2_SCALE)
    return (grown * (1.0 / jnp.sum(grown, axis=-1, keepdims=True))).astype(jnp.bfloat16)


def forward_kernel(
    dev_ref, counts_ref, bq, bk, bv, sq, sk, sv, image_ref, owner_ref, w_ref,
    big_out, slots_out, score_out,
    image_s, columns_s, place_s, big_class_s, small_class_s, rows_s,
):
    big_rows = bq.shape[0]
    small_rows = sq.shape[0]
    slot_rows = slots_out.shape[0]
    head = pl.program_id(0)
    ends = image_ends(counts_ref)

    @pl.when(head == 0)
    def _():
        image, dest, columns = small_tables(dev_ref[0], image_ref, owner_ref)
        image_s[...] = jnp.broadcast_to(image, image_s.shape)
        columns_s[...] = columns
        for start in range(0, slot_rows, BLOCK):
            place_s[start : start + BLOCK, :] = (
                (iota((BLOCK, small_rows), 0) + start == dest)
                .astype(jnp.float32)
                .astype(jnp.bfloat16)
            )
        big_class_s[...] = class_mask_big(big_rows, counts_ref)
        small_class_s[...] = class_mask_small(columns)
        score_out[...] = jnp.zeros_like(score_out)

    weight = w_ref[...]
    score = jnp.zeros((1, LANES), jnp.float32)
    for q0, k0 in windows(small_rows):
        image_col = columns_s[q0 : q0 + BLOCK, 0:1].astype(jnp.int32)
        allowed = image_col == image_s[0:1, k0 : k0 + WINDOW]
        weights = probs(sq[q0 : q0 + BLOCK, :], sk[k0 : k0 + WINDOW, :], allowed)
        out = mm(weights, sv[k0 : k0 + WINDOW, :]).astype(jnp.bfloat16)
        rows_s[q0 : q0 + BLOCK, :] = out
        dotted = jnp.sum(out.astype(jnp.float32) * weight, axis=1, keepdims=True)
        score = score + jnp.sum(
            dotted * small_class_s[q0 : q0 + BLOCK, :], axis=0, keepdims=True
        )
    placed = rows_s[...]
    for start in range(0, slot_rows, 256):
        slots_out[start : start + 256, :] = mm(place_s[start : start + 256, :], placed).astype(
            jnp.bfloat16
        )
    segment_row = segment_of(iota((1, big_rows), 1), ends)
    for q0 in range(0, big_rows, BLOCK):
        segment_col = segment_of(iota((BLOCK, 1), 0) + q0, ends)
        weights = probs(bq[q0 : q0 + BLOCK, :], bk[...], segment_col == segment_row)
        out = mm(weights, bv[...]).astype(jnp.bfloat16)
        big_out[q0 : q0 + BLOCK, :] = out
        dotted = jnp.sum(out.astype(jnp.float32) * weight, axis=1, keepdims=True)
        score = score + jnp.sum(
            dotted * big_class_s[q0 : q0 + BLOCK, :], axis=0, keepdims=True
        )
    score_out[...] += score


def pick(table, number, first_small):
    is_big = number < first_small
    small = number - first_small
    small_dev = (small * 21846) >> 20
    device = jnp.where(is_big, number >> 2, small_dev)
    lane = jnp.where(is_big, number & 3, BIG_IMG + small - MIG_IMG * small_dev)
    count = number.shape[1]
    chosen = (iota((table.shape[1], count), 0) == device).astype(jnp.float32)
    spread = jnp.dot(
        table,
        chosen,
        preferred_element_type=jnp.float32,
        precision=lax.Precision.HIGHEST,
    )
    return jnp.sum(
        jnp.where(iota(spread.shape, 0) == lane, spread, 0.0), axis=0, keepdims=True
    )


def backward_block(q, k, v, cot, allowed):
    weights = probs(q, k, allowed)
    wide = weights.astype(jnp.float32)
    weight_grad = mm_nt(cot, v)
    row_dot = jnp.sum(wide * weight_grad, axis=-1, keepdims=True)
    score_grad = (wide * (weight_grad - row_dot)).astype(jnp.bfloat16)
    return weights, score_grad


def backward_kernel(
    dev_ref, counts_ref, bq, bk, bv, bd, sq, sk, sv, sd, image_ref, owner_ref, w_ref,
    gathered_ref, pairs_ref,
    big_dq, big_dk, big_dv, small_dq, small_dk, small_dv, loss_out,
    image_s, columns_s, take_s, big_gain_s, small_gain_s, cot_s, dk_s, dv_s,
):
    big_rows = bq.shape[0]
    small_rows = sq.shape[0]
    slot_rows = sd.shape[0]
    head = pl.program_id(0)
    ends = image_ends(counts_ref)

    @pl.when(head == 0)
    def _():
        dev = dev_ref[0]
        image, _, columns = small_tables(dev, image_ref, owner_ref)
        image_s[...] = jnp.broadcast_to(image, image_s.shape)
        columns_s[...] = columns
        dest_col = columns[:, 2:3].astype(jnp.int32)
        for start in range(0, slot_rows, 256):
            take_s[:, start : start + 256] = (
                (iota((small_rows, 256), 1) + start == dest_col)
                .astype(jnp.float32)
                .astype(jnp.bfloat16)
            )
        first_small = gathered_ref.shape[0] * BIG_IMG
        table = jnp.transpose(gathered_ref[...])[0:56, :]
        preferred = pairs_ref[0:1, :]
        rejected = pairs_ref[1:2, :]
        margin = pick(table, rejected, first_small) - pick(table, preferred, first_small)
        small_exp = jnp.exp(-jnp.abs(margin))
        loss_out[...] = jnp.maximum(margin, 0.0) + jnp.log1p(small_exp)
        pull = jnp.where(margin >= 0, 1.0, small_exp) / (1.0 + small_exp)
        lane = iota((LANES, 1), 0)
        number = jnp.where(
            lane < BIG_IMG,
            dev * BIG_IMG + lane,
            jnp.where(lane < IMAGES, first_small + dev * MIG_IMG + lane - BIG_IMG, -1),
        )
        gain = jnp.sum(
            jnp.where(rejected == number, pull, 0.0)
            - jnp.where(preferred == number, pull, 0.0),
            axis=1,
            keepdims=True,
        )
        gain_row = jnp.transpose(jnp.broadcast_to(gain, (LANES, LANES)))[0:1, :]
        big_gain_s[...] = jnp.broadcast_to(
            jnp.sum(class_mask_big(big_rows, counts_ref) * gain_row, axis=1, keepdims=True),
            big_gain_s.shape,
        )
        small_gain_s[...] = jnp.broadcast_to(
            jnp.sum(class_mask_small(columns) * gain_row, axis=1, keepdims=True),
            small_gain_s.shape,
        )

    weight = w_ref[...]
    dk_s[...] = jnp.zeros_like(dk_s)
    dv_s[...] = jnp.zeros_like(dv_s)
    segment_row = segment_of(iota((1, big_rows), 1), ends)
    for q0 in range(0, big_rows, BLOCK):
        span = slice(q0, q0 + BLOCK)
        segment_col = segment_of(iota((BLOCK, 1), 0) + q0, ends)
        cot = (bd[span, :].astype(jnp.float32) + big_gain_s[span, :] * weight).astype(
            jnp.bfloat16
        )
        weights, score_grad = backward_block(
            bq[span, :], bk[...], bv[...], cot, segment_col == segment_row
        )
        big_dq[span, :] = (mm(score_grad, bk[...]) * SCALE).astype(jnp.bfloat16)
        dk_s[...] += mm_tn(score_grad, bq[span, :])
        dv_s[...] += mm_tn(weights, cot)
    big_dk[...] = (dk_s[...] * SCALE).astype(jnp.bfloat16)
    big_dv[...] = dv_s[...].astype(jnp.bfloat16)

    for start in range(0, small_rows, BLOCK):
        span = slice(start, start + BLOCK)
        cot_s[span, :] = (
            mm(take_s[span, :], sd[...]) + small_gain_s[span, :] * weight
        ).astype(jnp.bfloat16)
    small_span = slice(0, small_rows)
    dk_s[small_span, :] = jnp.zeros((small_rows, HD), jnp.float32)
    dv_s[small_span, :] = jnp.zeros((small_rows, HD), jnp.float32)
    for q0, k0 in windows(small_rows):
        span = slice(q0, q0 + BLOCK)
        keys = slice(k0, k0 + WINDOW)
        image_col = columns_s[span, 0:1].astype(jnp.int32)
        allowed = image_col == image_s[0:1, keys]
        cot = cot_s[span, :]
        weights, score_grad = backward_block(sq[span, :], sk[keys, :], sv[keys, :], cot, allowed)
        small_dq[span, :] = (mm(score_grad, sk[keys, :]) * SCALE).astype(jnp.bfloat16)
        dk_s[keys, :] += mm_tn(score_grad, sq[span, :])
        dv_s[keys, :] += mm_tn(weights, cot)
    small_dk[...] = (dk_s[small_span, :] * SCALE).astype(jnp.bfloat16)
    small_dv[...] = dv_s[small_span, :].astype(jnp.bfloat16)


def gather_scores(score):
    members = lax.axis_size("mp")
    step = 1
    while step < members:
        score = score + lax.ppermute(score, "mp", [(i, i ^ step) for i in range(members)])
        step *= 2
    devices = lax.axis_size("dp")
    index = lax.axis_index("dp")
    step = 1
    while step < devices:
        other = lax.ppermute(score, "dp", [(i, i ^ step) for i in range(devices)])
        upper = (index // step) % 2 == 1
        score = jnp.where(
            upper, jnp.concatenate([other, score]), jnp.concatenate([score, other])
        )
        step *= 2
    return score


def on_device(
    big_q, big_k, big_v, big_dout, big_counts, small_q, small_k, small_v,
    small_image, owner, owner_dout, reward_w, pair_perm,
):
    features = big_q.shape[1]
    heads = features // HD
    big_rows = big_q.shape[0]
    small_rows = small_q.shape[0]
    slot_rows = owner_dout.shape[0]
    bf16 = jnp.bfloat16
    dev = lax.axis_index("dp").astype(jnp.int32).reshape(1)
    counts = big_counts.reshape(-1)
    weight = reward_w.reshape(1, -1)
    pairs = pair_perm.reshape(-1, 2).T

    returned = lax.all_to_all(owner_dout, "dp", split_axis=0, concat_axis=0, tiled=True)

    def by_head(rows):
        return pl.BlockSpec((rows, HD), lambda h, d, c: (0, h))

    def whole(shape):
        return pl.BlockSpec(shape, lambda h, d, c: (0, 0))

    image_spec = pl.BlockSpec((8, small_rows), lambda h, d, c: (d[0] // 8, 0))
    owner_spec = pl.BlockSpec((MIG_IMG, 1), lambda h, d, c: (d[0], 0))
    big_flops = 2 * big_rows * big_rows * features
    small_flops = 2 * small_rows * WINDOW * features
    params = pltpu.CompilerParams(
        dimension_semantics=("arbitrary",), vmem_limit_bytes=56 * 2**20
    )

    big_out, slots, score = pl.pallas_call(
        forward_kernel,
        grid_spec=pltpu.PrefetchScalarGridSpec(
            num_scalar_prefetch=2,
            grid=(heads,),
            in_specs=[by_head(big_rows)] * 3
            + [by_head(small_rows)] * 3
            + [image_spec, owner_spec, by_head(1)],
            out_specs=[by_head(big_rows), by_head(slot_rows), whole((1, LANES))],
            scratch_shapes=[
                pltpu.VMEM((8, small_rows), jnp.int32),
                pltpu.VMEM((small_rows, LANES), jnp.float32),
                pltpu.VMEM((slot_rows, small_rows), bf16),
                pltpu.VMEM((big_rows, LANES), jnp.float32),
                pltpu.VMEM((small_rows, LANES), jnp.float32),
                pltpu.VMEM((small_rows, HD), bf16),
            ],
        ),
        out_shape=[
            jax.ShapeDtypeStruct((big_rows, features), bf16),
            jax.ShapeDtypeStruct((slot_rows, features), bf16),
            jax.ShapeDtypeStruct((1, LANES), jnp.float32),
        ],
        compiler_params=params,
        cost_estimate=pl.CostEstimate(
            flops=2 * big_flops + 2 * small_flops + 2 * slot_rows * small_rows * features,
            bytes_accessed=2 * features * (4 * big_rows + 3 * small_rows + slot_rows),
            transcendentals=heads * (big_rows * big_rows + small_rows * WINDOW),
        ),
    )(dev, counts, big_q, big_k, big_v, small_q, small_k, small_v, small_image, owner, weight)

    gathered = gather_scores(score)
    small_out = lax.all_to_all(slots, "dp", split_axis=0, concat_axis=0, tiled=True)

    pair_count = pairs.shape[1]
    grads = pl.pallas_call(
        backward_kernel,
        grid_spec=pltpu.PrefetchScalarGridSpec(
            num_scalar_prefetch=2,
            grid=(heads,),
            in_specs=[by_head(big_rows)] * 4
            + [by_head(small_rows)] * 3
            + [by_head(slot_rows), image_spec, owner_spec, by_head(1)]
            + [whole(gathered.shape), whole(pairs.shape)],
            out_specs=[by_head(big_rows)] * 3
            + [by_head(small_rows)] * 3
            + [whole((1, pair_count))],
            scratch_shapes=[
                pltpu.VMEM((8, small_rows), jnp.int32),
                pltpu.VMEM((small_rows, LANES), jnp.float32),
                pltpu.VMEM((small_rows, slot_rows), bf16),
                pltpu.VMEM((big_rows, LANES), jnp.float32),
                pltpu.VMEM((small_rows, LANES), jnp.float32),
                pltpu.VMEM((small_rows, HD), bf16),
                pltpu.VMEM((big_rows, HD), jnp.float32),
                pltpu.VMEM((big_rows, HD), jnp.float32),
            ],
        ),
        out_shape=[jax.ShapeDtypeStruct((big_rows, features), bf16)] * 3
        + [jax.ShapeDtypeStruct((small_rows, features), bf16)] * 3
        + [jax.ShapeDtypeStruct((1, pair_count), jnp.float32)],
        compiler_params=params,
        cost_estimate=pl.CostEstimate(
            flops=5 * big_flops + 5 * small_flops + 2 * slot_rows * small_rows * features,
            bytes_accessed=2 * features * (7 * big_rows + 6 * small_rows + slot_rows),
            transcendentals=heads * (big_rows * big_rows + small_rows * WINDOW),
        ),
    )(
        dev, counts, big_q, big_k, big_v, big_dout, small_q, small_k, small_v, returned,
        small_image, owner, weight, gathered, pairs,
    )
    big_dq, big_dk, big_dv, small_dq, small_dk, small_dv, loss = grads
    small_out, loss = lax.optimization_barrier((small_out, loss))
    return (
        big_out, small_out, big_dq, big_dk, big_dv, small_dq, small_dk, small_dv,
        loss.reshape(-1),
    )


def solution(mesh):
    rows = P("dp", "mp")
    return jax.shard_map(
        on_device,
        mesh=mesh,
        in_specs=(
            rows, rows, rows, rows, P("dp", None), rows, rows, rows, P(), P(), rows,
            P("mp"), P(),
        ),
        out_specs=(rows, rows, rows, rows, rows, rows, rows, rows, P()),
        check_vma=False,
    )
```

time: 458 us -> 146 us (0.32)
  the two profiles are of different devices: /device:TPU:1 before, /device:TPU:6 now
where the time goes in v1:
time: 146 us; the launch traced here: 145 us
  Pallas kernels  60.1 us (41%)
  waiting for transfers between devices  42.7 us (29%)
  starting transfers between devices  33.8 us (23%)
  local copies, waits for them, and re-layouts  6.11 us (4%)
  other arithmetic  1.96 us (1%)
    pallas_call x1, Pallas kernels, on_device(): pl.pallas_call(backward_kernel, grid_spec=pltpu.PrefetchScalarGridSpec(nu...  36.6 us
    ppermute x6, waiting for transfers between devices, gather_scores(): other = lax.ppermute(score, 'dp', [(i, i ^ step) for i in range(devices)])  32.5 us
    pallas_call x1, Pallas kernels, on_device(): pl.pallas_call(forward_kernel, grid_spec=pltpu.PrefetchScalarGridSpec(num...  23.5 us
    all_to_all x1, starting transfers between devices, on_device(): lax.all_to_all(owner_dout, 'dp', split_axis=0, concat_axis=0, tiled=True)  12.3 us
    ppermute x6, starting transfers between devices, gather_scores(): other = lax.ppermute(score, 'dp', [(i, i ^ step) for i in range(devices)])  8.61 us
    all_to_all x1, starting transfers between devices, on_device(): lax.all_to_all(slots, 'dp', split_axis=0, concat_axis=0, tiled=True)  8.05 us
    all_to_all x1, waiting for transfers between devices, on_device(): lax.all_to_all(owner_dout, 'dp', split_axis=0, concat_axis=0, tiled=True)  6.46 us
    ppermute x2, starting transfers between devices, gather_scores(): lax.ppermute(score, 'mp', [(i, i ^ step) for i in range(members)])  4.86 us
  transfers between devices with their start and end apart: 10, of which 9 were waited for; matrix products, arithmetic and copies ran while one was open for 3% of the time, Pallas kernels for 41%

profile of v1, /device:TPU:6, one launch (start us, length us, event | category | flops | bytes accessed | tf_op | source)
XLA Modules:
  0.0 145.5 jit_solution(12405892373777610948)
XLA Ops:
  0.6 0.0 copy-start.3
  0.7 0.0 copy-start.2
  0.7 12.3 %all-to-all-start.1 = ((bf16[64,16,640]{2,1,0:T(8,128)(2,1)}), bf16[64,16,640]{2,1,0:T(8,128)(2,1)S(1)}, u32[]{:S(2)}, u32[]{:S(2)}) async-start(bf16[64,16,640]{2,1,0:T(8,128)(2,1)} %bitcast.8), calls=%async_computation.1 | async-start | bytes 2621440 | tf_op jit(solution)/shard_map/all_to_all | solution.py:328
  13.0 0.6 reshape.39.w_ref
  13.6 1.7 %copy.24.owner_ref = s32[3072,1]{1,0:T(8,128)} copy(s32[3072,1]{0,1:T(1,128)S(1)} %copy-done.2) | data formatting | bytes 24576 | tf_op args[9]
  15.3 23.5 %shard_map.196 = (bf16[640,640]{1,0:T(8,128)(2,1)}, bf16[1024,640]{1,0:T(8,128)(2,1)}, f32[1,128]{1,0:T(1,128)}) custom-call(s32[1]{0:T(128)} %bitcast.dev_ref, s32[4]{0:T(128)} %bitcast.12, bf16[640,640]{1,0:T(8,128)(2,1)} %bq.3, bf16[640,640]{1,0:T(8,128)(2,1)} %bk.3, bf16[640,640]{1,0:T(8,128)(2,1)} %bv.3, bf16[512,640]{1,0:T(8,128)(2,1)} %sq.3, ...), custom_call_target="tpu_custom_call" | custom-call | flops 2055208960 | bytes 6553600 | tf_op jit(solution)/shard_map/pallas_call | solution.py:344
  38.8 6.5 %all-to-all-done.1 = bf16[64,16,640]{2,1,0:T(8,128)(2,1)S(1)} async-done(((bf16[64,16,640]{2,1,0:T(8,128)(2,1)}), bf16[64,16,640]{2,1,0:T(8,128)(2,1)S(1)}, u32[]{:S(2)}, u32[]{:S(2)}) %all-to-all-start.1) | async-done | bytes 1310752 | tf_op jit(solution)/shard_map/all_to_all | solution.py:328
  45.3 1.1 copy-done
  46.3 8.1 %all-to-all-start = ((bf16[64,16,640]{2,1,0:T(8,128)(2,1)}), bf16[64,16,640]{2,1,0:T(8,128)(2,1)S(1)}, u32[]{:S(2)}, u32[]{:S(2)}) async-start(bf16[64,16,640]{2,1,0:T(8,128)(2,1)} %bitcast.10), calls=%async_computation | async-start | bytes 2621440 | tf_op jit(solution)/shard_map/all_to_all | solution.py:376
  54.4 1.7 %collective-permute-start = (f32[1,128]{1,0:T(1,128)S(1)}, f32[1,128]{1,0:T(1,128)S(1)}, u32[]{:S(2)}, u32[]{:S(2)}) collective-permute-start(f32[1,128]{1,0:T(1,128)S(1)} %copy-done.4), channel_id=1, source_target_pairs={{0,1},{1,0},{2,3},{3,2},{4,5},{5,4},{6,7},{7,6},{8,9},{9,8},{10,11... | collective-permute-start | bytes 1544 | tf_op jit(solution)/shard_map/ppermute | solution.py:298
  56.1 2.0 %collective-permute-done = f32[1,128]{1,0:T(1,128)S(1)} collective-permute-done((f32[1,128]{1,0:T(1,128)S(1)}, f32[1,128]{1,0:T(1,128)S(1)}, u32[]{:S(2)}, u32[]{:S(2)}) %collective-permute-start) | collective-permute-done | bytes 544 | tf_op jit(solution)/shard_map/ppermute | solution.py:298
  58.0 3.2 %collective-permute-start.1 = (f32[1,128]{1,0:T(1,128)S(1)}, f32[1,128]{1,0:T(1,128)S(1)}, u32[]{:S(2)}, u32[]{:S(2)}) collective-permute-start(f32[1,128]{1,0:T(1,128)S(1)} %add.37), channel_id=1, source_target_pairs={{0,2},{1,3},{2,0},{3,1},{4,6},{5,7},{6,4},{7,5},{8,10},{9,11},{10,... | collective-permute-start | bytes 1544 | tf_op jit(solution)/shard_map/ppermute | solution.py:298
  61.2 1.9 %collective-permute-done.1 = f32[1,128]{1,0:T(1,128)S(1)} collective-permute-done((f32[1,128]{1,0:T(1,128)S(1)}, f32[1,128]{1,0:T(1,128)S(1)}, u32[]{:S(2)}, u32[]{:S(2)}) %collective-permute-start.1) | collective-permute-done | bytes 544 | tf_op jit(solution)/shard_map/ppermute | solution.py:298
  63.1 0.0 collective-permute-start.2
  63.1 1.1 collective-permute-done.2
  64.2 1.6 %collective-permute-start.3 = (f32[2,128]{1,0:T(2,128)S(1)}, f32[2,128]{1,0:T(2,128)S(1)}, u32[]{:S(2)}, u32[]{:S(2)}) collective-permute-start(f32[2,128]{1,0:T(2,128)S(1)} %maximum_select_fusion.5), channel_id=1, source_target_pairs={{0,8},{4,12},{8,0},{12,4},{16,24},{20,28},{24,16},{28,20},{32,40},... | collective-permute-start | bytes 3080 | tf_op jit(solution)/shard_map/ppermute | solution.py:304
  65.8 19.0 %collective-permute-done.3 = f32[2,128]{1,0:T(2,128)S(1)} collective-permute-done((f32[2,128]{1,0:T(2,128)S(1)}, f32[2,128]{1,0:T(2,128)S(1)}, u32[]{:S(2)}, u32[]{:S(2)}) %collective-permute-start.3) | collective-permute-done | bytes 1056 | tf_op jit(solution)/shard_map/ppermute | solution.py:304
  84.8 0.5 collective-permute-start.4
  85.3 4.1 %collective-permute-done.4 = f32[4,128]{1,0:T(4,128)S(1)} collective-permute-done((f32[4,128]{1,0:T(4,128)S(1)}, f32[4,128]{1,0:T(4,128)S(1)}, u32[]{:S(2)}, u32[]{:S(2)}) %collective-permute-start.4) | collective-permute-done | bytes 2080 | tf_op jit(solution)/shard_map/ppermute | solution.py:304
  89.4 4.6 %collective-permute-start.5 = (f32[8,128]{1,0:T(8,128)S(1)}, f32[8,128]{1,0:T(8,128)S(1)}, u32[]{:S(2)}, u32[]{:S(2)}) collective-permute-start(f32[8,128]{1,0:T(8,128)S(1)} %maximum_select_fusion.3), channel_id=1, source_target_pairs={{0,32},{4,36},{8,40},{12,44},{16,48},{20,52},{24,56},{28,60},{32,0... | collective-permute-start | bytes 12296 | tf_op jit(solution)/shard_map/ppermute | solution.py:304
  94.0 3.0 %collective-permute-done.5 = f32[8,128]{1,0:T(8,128)S(1)} collective-permute-done((f32[8,128]{1,0:T(8,128)S(1)}, f32[8,128]{1,0:T(8,128)S(1)}, u32[]{:S(2)}, u32[]{:S(2)}) %collective-permute-start.5) | collective-permute-done | bytes 4128 | tf_op jit(solution)/shard_map/ppermute | solution.py:304
  97.0 0.7 collective-permute-start.6
  97.8 2.9 %collective-permute-done.6 = f32[16,128]{1,0:T(8,128)S(1)} collective-permute-done((f32[16,128]{1,0:T(8,128)S(1)}, f32[16,128]{1,0:T(8,128)S(1)}, u32[]{:S(2)}, u32[]{:S(2)}) %collective-permute-start.6) | collective-permute-done | bytes 8224 | tf_op jit(solution)/shard_map/ppermute | solution.py:304
  100.7 1.2 collective-permute-start.7
  101.9 0.8 reshape.40
  102.7 0.9 copy.25
  103.6 2.3 %collective-permute-done.7 = f32[32,128]{1,0:T(8,128)S(1)} collective-permute-done((f32[32,128]{1,0:T(8,128)S(1)}, f32[32,128]{1,0:T(8,128)S(1)}, u32[]{:S(2)}, u32[]{:S(2)}) %collective-permute-start.7) | collective-permute-done | bytes 16416 | tf_op jit(solution)/shard_map/ppermute | solution.py:304
  105.9 0.6 maximum_select_fusion.gathered_ref
  106.5 36.6 %shard_map.197 = (bf16[640,640]{1,0:T(8,128)(2,1)}, bf16[640,640]{1,0:T(8,128)(2,1)}, bf16[640,640]{1,0:T(8,128)(2,1)}, bf16[512,640]{1,0:T(8,128)(2,1)}, bf16[5...) custom-call(s32[1]{0:T(128)} %bitcast.dev_ref, s32[4]{0:T(128)} %bitcast.13, bf16[640,640]{1,0:T(8,128)(2,1)} %bq.3, ...), custom_call_target="tpu_custom_call" | custom-call | flops 4131389440 | bytes 10977280 | tf_op jit(solution)/shard_map/pallas_call | solution.py:379
  143.1 0.0 all-to-all-done
  143.1 1.3 reduce
  144.4 1.1 copy.28
  (14 shorter events, 0.1 us)
Async XLA Ops:
  0.6 12.3 %copy-start.3 = (f32[640]{0:T(1024)S(1)}, f32[640]{0:T(1024)}, u32[]{:S(2)}) copy-start(f32[640]{0:T(1024)} %param.24) | copy-start | bytes 7684
  0.7 12.9 %copy-start.2 = (s32[3072,1]{0,1:T(1,128)S(1)}, s32[3072,1]{0,1:T(1,128)}, u32[]{:S(2)}) copy-start(s32[3072,1]{0,1:T(1,128)} %param.22) | copy-start | bytes 36868
  0.7 44.6 %all-to-all-start.1 = ((bf16[64,16,640]{2,1,0:T(8,128)(2,1)}), bf16[64,16,640]{2,1,0:T(8,128)(2,1)S(1)}, u32[]{:S(2)}, u32[]{:S(2)}) async-start(bf16[64,16,640]{2,1,0:T(8,128)(2,1)} %bitcast.8), calls=%async_computation.1 | async-start | bytes 2621440 | tf_op jit(solution)/shard_map/all_to_all | solution.py:328
  45.3 1.1 copy-start
  45.3 9.1 %copy-start.4 = (f32[1,128]{1,0:T(1,128)S(1)}, f32[1,128]{1,0:T(1,128)}, u32[]{:S(2)}) copy-start(f32[1,128]{1,0:T(1,128)} %get-tuple-element.23) | copy-start | bytes 1540
  45.3 56.6 %copy-start.1 = (s32[3328]{0:T(1024)S(1)}, s32[3328]{0:T(1024)}, u32[]{:S(2)}) copy-start(s32[3328]{0:T(1024)} %param.25) | copy-start | bytes 39940
  46.3 96.7 %all-to-all-start = ((bf16[64,16,640]{2,1,0:T(8,128)(2,1)}), bf16[64,16,640]{2,1,0:T(8,128)(2,1)S(1)}, u32[]{:S(2)}, u32[]{:S(2)}) async-start(bf16[64,16,640]{2,1,0:T(8,128)(2,1)} %bitcast.10), calls=%async_computation | async-start | bytes 2621440 | tf_op jit(solution)/shard_map/all_to_all | solution.py:376
  54.4 3.6 %collective-permute-start = (f32[1,128]{1,0:T(1,128)S(1)}, f32[1,128]{1,0:T(1,128)S(1)}, u32[]{:S(2)}, u32[]{:S(2)}) collective-permute-start(f32[1,128]{1,0:T(1,128)S(1)} %copy-done.4), channel_id=1, source_target_pairs={{0,1},{1,0},{2,3},{3,2},{4,5},{5,4},{6,7},{7,6},{8,9},{9,8},{10,11... | collective-permute-start | bytes 1544 | tf_op jit(solution)/shard_map/ppermute | solution.py:298
  58.0 5.0 %collective-permute-start.1 = (f32[1,128]{1,0:T(1,128)S(1)}, f32[1,128]{1,0:T(1,128)S(1)}, u32[]{:S(2)}, u32[]{:S(2)}) collective-permute-start(f32[1,128]{1,0:T(1,128)S(1)} %add.37), channel_id=1, source_target_pairs={{0,2},{1,3},{2,0},{3,1},{4,6},{5,7},{6,4},{7,5},{8,10},{9,11},{10,... | collective-permute-start | bytes 1544 | tf_op jit(solution)/shard_map/ppermute | solution.py:298
  63.1 1.1 collective-permute-start.2
  64.2 20.6 %collective-permute-start.3 = (f32[2,128]{1,0:T(2,128)S(1)}, f32[2,128]{1,0:T(2,128)S(1)}, u32[]{:S(2)}, u32[]{:S(2)}) collective-permute-start(f32[2,128]{1,0:T(2,128)S(1)} %maximum_select_fusion.5), channel_id=1, source_target_pairs={{0,8},{4,12},{8,0},{12,4},{16,24},{20,28},{24,16},{28,20},{32,40},... | collective-permute-start | bytes 3080 | tf_op jit(solution)/shard_map/ppermute | solution.py:304
  84.8 4.6 %collective-permute-start.4 = (f32[4,128]{1,0:T(4,128)S(1)}, f32[4,128]{1,0:T(4,128)S(1)}, u32[]{:S(2)}, u32[]{:S(2)}) collective-permute-start(f32[4,128]{1,0:T(4,128)S(1)} %maximum_select_fusion.4), channel_id=1, source_target_pairs={{0,16},{4,20},{8,24},{12,28},{16,0},{20,4},{24,8},{28,12},{32,48},... | collective-permute-start | bytes 6152 | tf_op jit(solution)/shard_map/ppermute | solution.py:304
  89.4 7.6 %collective-permute-start.5 = (f32[8,128]{1,0:T(8,128)S(1)}, f32[8,128]{1,0:T(8,128)S(1)}, u32[]{:S(2)}, u32[]{:S(2)}) collective-permute-start(f32[8,128]{1,0:T(8,128)S(1)} %maximum_select_fusion.3), channel_id=1, source_target_pairs={{0,32},{4,36},{8,40},{12,44},{16,48},{20,52},{24,56},{28,60},{32,0... | collective-permute-start | bytes 12296 | tf_op jit(solution)/shard_map/ppermute | solution.py:304
  97.0 3.7 %collective-permute-start.6 = (f32[16,128]{1,0:T(8,128)S(1)}, f32[16,128]{1,0:T(8,128)S(1)}, u32[]{:S(2)}, u32[]{:S(2)}) collective-permute-start(f32[16,128]{1,0:T(8,128)S(1)} %maximum_select_fusion.2), channel_id=1, source_target_pairs={{0,64},{4,68},{8,72},{12,76},{16,80},{20,84},{24,88},{28,92},{32,9... | collective-permute-start | bytes 24584 | tf_op jit(solution)/shard_map/ppermute | solution.py:304
  100.7 5.2 %collective-permute-start.7 = (f32[32,128]{1,0:T(8,128)S(1)}, f32[32,128]{1,0:T(8,128)S(1)}, u32[]{:S(2)}, u32[]{:S(2)}) collective-permute-start(f32[32,128]{1,0:T(8,128)S(1)} %maximum_select_fusion.1), channel_id=1, source_target_pairs={{0,128},{4,132},{8,136},{12,140},{16,144},{20,148},{24,152},{28,15... | collective-permute-start | bytes 49160 | tf_op jit(solution)/shard_map/ppermute | solution.py:304

commit v2 on v1

v2 whole, which is shorter than its diff:
```python
import functools
import math

import jax
import jax.numpy as jnp
from jax import lax
from jax.experimental import pallas as pl
from jax.experimental.pallas import tpu as pltpu
from jax.sharding import PartitionSpec as P

HD = 128
BIG_IMG = 4
MIG_IMG = 48
SMALL = 16
LANES = 128
IMAGES = BIG_IMG + MIG_IMG
SCALE = 1.0 / math.sqrt(HD)
EXP2_SCALE = SCALE * math.log2(math.e)
BLOCK = 128
WINDOW = 256
MASKED = -1e30
X, Z = 4, 8


def mm(left, right):
    return jnp.dot(left, right, preferred_element_type=jnp.float32)


def mm_nt(left, right):
    return lax.dot_general(
        left, right, (((1,), (1,)), ((), ())), preferred_element_type=jnp.float32
    )


def mm_tn(left, right):
    return lax.dot_general(
        left, right, (((0,), (0,)), ((), ())), preferred_element_type=jnp.float32
    )


def iota(shape, dim):
    return lax.broadcasted_iota(jnp.int32, shape, dim)


def windows(rows):
    pairs = []
    for start in range(0, rows, BLOCK):
        pairs.append((start, min(max(start - (WINDOW - BLOCK) // 2, 0), rows - WINDOW)))
    return pairs


def image_ends(counts):
    first = counts[0]
    second = first + counts[1]
    third = second + counts[2]
    return first, second, third


def segment_of(rows, ends):
    return sum((rows >= end).astype(jnp.int32) for end in ends)


def class_mask_big(rows, counts):
    ends = image_ends(counts)
    lane = iota((rows, LANES), 1)
    start = jnp.where(
        lane == 0,
        0,
        jnp.where(
            lane == 1,
            ends[0],
            jnp.where(lane == 2, ends[1], jnp.where(lane == 3, ends[2], -1)),
        ),
    )
    return (iota((rows, LANES), 0) == start).astype(jnp.float32)


def small_tables(dev, image_ref, owner_ref):
    image = image_ref[pl.ds(lax.rem(dev, 8), 1), :]
    rows = image.shape[1]
    image_f = image.astype(jnp.float32)
    image_col = jnp.transpose(jnp.broadcast_to(image_f, (LANES, rows)))
    before = jnp.zeros((1, rows), jnp.float32)
    for start in range(0, rows, LANES):
        column = image_col[start : start + LANES, 0:1]
        before = before + jnp.sum(
            (column < image_f).astype(jnp.float32), axis=0, keepdims=True
        )
    position = iota((1, rows), 1).astype(jnp.float32) - before
    first = dev * MIG_IMG
    line = first // LANES
    last = owner_ref.shape[0] - 1
    lane = iota((LANES, LANES), 1)
    near = jnp.broadcast_to(owner_ref[pl.ds(line, 1), :], (LANES, LANES))
    far = jnp.broadcast_to(
        owner_ref[pl.ds(jnp.minimum(line + 1, last), 1), :], (LANES, LANES)
    )
    wanted = first - line * LANES + iota((LANES, LANES), 0)
    owners = jnp.sum(
        jnp.where(lane == wanted, near, 0) + jnp.where(lane + LANES == wanted, far, 0),
        axis=1,
        keepdims=True,
    )[0:MIG_IMG, :].astype(jnp.float32)
    hot = iota((MIG_IMG, rows), 0) == image
    owner_row = jnp.sum(jnp.where(hot, owners, 0.0), axis=0, keepdims=True)
    dest = owner_row * SMALL + position
    sub = iota((LANES, rows), 0)
    stacked = jnp.where(sub == 0, image_f, jnp.where(sub == 1, position, dest))
    columns = jnp.transpose(stacked)
    return image, dest.astype(jnp.int32), columns


def class_mask_small(columns):
    lane = iota(columns.shape, 1)
    image = columns[:, 0:1].astype(jnp.int32)
    first = columns[:, 1:2] == 0.0
    return ((image + BIG_IMG == lane) & first).astype(jnp.float32)


def probs(queries, keys, allowed):
    return softmax(mm_nt(queries, keys), allowed)


def softmax(products, allowed):
    scores = jnp.where(allowed, products, MASKED)
    top = jnp.max(scores, axis=-1, keepdims=True)
    grown = jnp.exp2((scores - top) * EXP2_SCALE)
    return (grown * (1.0 / jnp.sum(grown, axis=-1, keepdims=True))).astype(jnp.bfloat16)


def heads_of(ref):
    return [slice(start, start + HD) for start in range(0, ref.shape[1], HD)]


def score_kernel(dev_ref, counts_ref, bq, bk, bv, sq, sk, sv, image_ref, w_ref, score_out):
    big_rows = bq.shape[0]
    small_rows = sq.shape[0]
    ends = image_ends(counts_ref)
    heads = heads_of(bq)
    image = image_ref[pl.ds(lax.rem(dev_ref[0], 8), 1), :]
    number = iota((64, 1), 0)
    start = jnp.sum((image < number - BIG_IMG).astype(jnp.int32), axis=1, keepdims=True)
    chosen = (iota((64, small_rows), 1) == start).astype(jnp.float32).astype(jnp.bfloat16)
    big_number = iota((SMALL, 1), 0)
    big_start = jnp.where(
        big_number == 0,
        0,
        jnp.where(big_number == 1, ends[0], jnp.where(big_number == 2, ends[1], ends[2])),
    )
    big_chosen = (iota((SMALL, big_rows), 1) == big_start).astype(jnp.float32)
    small_q = mm(chosen, sq[...]).astype(jnp.bfloat16)
    big_q = mm(big_chosen.astype(jnp.bfloat16), bq[...]).astype(jnp.bfloat16)
    segment_row = segment_of(iota((1, big_rows), 1), ends)
    small_mask = image == number - BIG_IMG
    big_mask = jnp.minimum(big_number, BIG_IMG - 1) == segment_row
    small_products = [mm_nt(small_q[:, h], sk[:, h]) for h in heads]
    big_products = [mm_nt(big_q[:, h], bk[:, h]) for h in heads]
    small_weights = [softmax(products, small_mask) for products in small_products]
    big_weights = [softmax(products, big_mask) for products in big_products]
    small_out = [mm(weights, sv[:, h]) for weights, h in zip(small_weights, heads)]
    big_out = [mm(weights, bv[:, h]) for weights, h in zip(big_weights, heads)]

    def dotted(parts):
        total = sum(
            part.astype(jnp.bfloat16).astype(jnp.float32) * w_ref[:, h]
            for part, h in zip(parts, heads)
        )
        return jnp.sum(total, axis=1, keepdims=True)

    lane = iota((64, LANES), 1)
    is_small = (lane == number) & (number >= BIG_IMG) & (number < IMAGES)
    big_lane = iota((SMALL, LANES), 1)
    is_big = (big_lane == big_number) & (big_number < BIG_IMG)
    score_out[...] = jnp.sum(
        jnp.where(is_small, dotted(small_out), 0.0), axis=0, keepdims=True
    ) + jnp.sum(jnp.where(is_big, dotted(big_out), 0.0), axis=0, keepdims=True)


def small_allowed(image_s, columns_s, rows):
    parts = []
    for q0, k0 in windows(rows):
        image_col = columns_s[q0 : q0 + BLOCK, 0:1].astype(jnp.int32)
        parts.append(image_col == image_s[0:1, k0 : k0 + WINDOW])
    return jnp.concatenate(parts, axis=0)


def small_products(left, right):
    return jnp.concatenate(
        [
            mm_nt(left[q0 : q0 + BLOCK, :], right[k0 : k0 + WINDOW, :])
            for q0, k0 in windows(left.shape[0])
        ],
        axis=0,
    )


def small_sums(left, right):
    return jnp.concatenate(
        [
            mm(left[q0 : q0 + BLOCK, :], right[k0 : k0 + WINDOW, :])
            for q0, k0 in windows(left.shape[0])
        ],
        axis=0,
    )


def small_kernel(dev_ref, sq, sk, sv, image_ref, owner_ref, slots_out):
    small_rows = sq.shape[0]
    slot_rows = slots_out.shape[0]
    heads = heads_of(sq)
    image, dest, columns = small_tables(dev_ref[0], image_ref, owner_ref)
    allowed = small_allowed(image, columns, small_rows)
    products = [small_products(sq[:, h], sk[:, h]) for h in heads]
    weights = [softmax(product, allowed) for product in products]
    out = jnp.concatenate(
        [small_sums(weight, sv[:, h]).astype(jnp.bfloat16) for weight, h in zip(weights, heads)],
        axis=1,
    )
    for start in range(0, slot_rows, 256):
        place = (iota((256, small_rows), 0) + start == dest).astype(jnp.float32)
        slots_out[start : start + 256, :] = mm(place.astype(jnp.bfloat16), out).astype(
            jnp.bfloat16
        )


def pick(table, image, first_small, dev):
    is_big = image < first_small
    small = image - first_small
    small_dev = (small * 21846) >> 20
    device = jnp.where(is_big, image >> 2, small_dev)
    row = gathered_row(device, dev)
    lane = jnp.where(is_big, image & 3, BIG_IMG + small - MIG_IMG * small_dev)
    count = image.shape[1]
    chosen = (iota((table.shape[1], count), 0) == row).astype(jnp.float32)
    spread = jnp.dot(
        table,
        chosen,
        preferred_element_type=jnp.float32,
        precision=lax.Precision.HIGHEST,
    )
    return jnp.sum(
        jnp.where(iota(spread.shape, 0) == lane, spread, 0.0), axis=0, keepdims=True
    )


def score_gradient(weights, weight_grad):
    wide = weights.astype(jnp.float32)
    row_dot = jnp.sum(wide * weight_grad, axis=-1, keepdims=True)
    return (wide * (weight_grad - row_dot)).astype(jnp.bfloat16)


def backward_kernel(
    dev_ref, counts_ref, bq, bk, bv, bd, sq, sk, sv, sd, image_ref, owner_ref, w_ref,
    near_ref, far_ref, pairs_ref,
    big_out, big_dq, big_dk, big_dv, small_dq, small_dk, small_dv, loss_out,
    image_s, columns_s, take_s, big_gain_s, small_gain_s, dk_s, dv_s,
):
    big_rows = bq.shape[0]
    small_rows = sq.shape[0]
    slot_rows = sd.shape[0]
    head = pl.program_id(0)
    ends = image_ends(counts_ref)

    @pl.when(head == 0)
    def _():
        dev = dev_ref[0]
        image, _, columns = small_tables(dev, image_ref, owner_ref)
        image_s[...] = jnp.broadcast_to(image, image_s.shape)
        columns_s[...] = columns
        dest_col = columns[:, 2:3].astype(jnp.int32)
        for start in range(0, slot_rows, 256):
            take_s[:, start : start + 256] = (
                (iota((small_rows, 256), 1) + start == dest_col)
                .astype(jnp.float32)
                .astype(jnp.bfloat16)
            )
        first_small = X * Z * 2 * BIG_IMG
        table = jnp.concatenate([near_ref[...], far_ref[...]])
        table = jnp.transpose(table)[0:56, :]
        preferred = pairs_ref[0:1, :]
        rejected = pairs_ref[1:2, :]
        margin = pick(table, rejected, first_small, dev) - pick(
            table, preferred, first_small, dev
        )
        small_exp = jnp.exp(-jnp.abs(margin))
        loss_out[...] = jnp.maximum(margin, 0.0) + jnp.log1p(small_exp)
        pull = jnp.where(margin >= 0, 1.0, small_exp) / (1.0 + small_exp)
        lane = iota((LANES, 1), 0)
        number = jnp.where(
            lane < BIG_IMG,
            dev * BIG_IMG + lane,
            jnp.where(lane < IMAGES, first_small + dev * MIG_IMG + lane - BIG_IMG, -1),
        )
        gain = jnp.sum(
            jnp.where(rejected == number, pull, 0.0)
            - jnp.where(preferred == number, pull, 0.0),
            axis=1,
            keepdims=True,
        )
        gain_row = jnp.transpose(jnp.broadcast_to(gain, (LANES, LANES)))[0:1, :]
        big_gain_s[...] = jnp.broadcast_to(
            jnp.sum(class_mask_big(big_rows, counts_ref) * gain_row, axis=1, keepdims=True),
            big_gain_s.shape,
        )
        small_gain_s[...] = jnp.broadcast_to(
            jnp.sum(class_mask_small(columns) * gain_row, axis=1, keepdims=True),
            small_gain_s.shape,
        )

    weight = w_ref[...]
    segment_row = segment_of(iota((1, big_rows), 1), ends)
    segment_col = segment_of(iota((big_rows, 1), 0), ends)
    cot = (bd[...].astype(jnp.float32) + big_gain_s[...] * weight).astype(jnp.bfloat16)
    weights = probs(bq[...], bk[...], segment_col == segment_row)
    big_out[...] = mm(weights, bv[...]).astype(jnp.bfloat16)
    score_grad = score_gradient(weights, mm_nt(cot, bv[...]))
    big_dq[...] = (mm(score_grad, bk[...]) * SCALE).astype(jnp.bfloat16)
    big_dk[...] = (mm_tn(score_grad, bq[...]) * SCALE).astype(jnp.bfloat16)
    big_dv[...] = mm_tn(weights, cot).astype(jnp.bfloat16)

    cot = (mm(take_s[...], sd[...]) + small_gain_s[...] * weight).astype(jnp.bfloat16)
    allowed = small_allowed(image_s, columns_s, small_rows)
    weights = softmax(small_products(sq, sk), allowed)
    score_grad = score_gradient(weights, small_products(cot, sv))
    small_dq[...] = (small_sums(score_grad, sk) * SCALE).astype(jnp.bfloat16)
    dk_s[...] = jnp.zeros_like(dk_s)
    dv_s[...] = jnp.zeros_like(dv_s)
    for q0, k0 in windows(small_rows):
        span = slice(q0, q0 + BLOCK)
        keys = slice(k0, k0 + WINDOW)
        dk_s[keys, :] += mm_tn(score_grad[span, :], sq[span, :])
        dv_s[keys, :] += mm_tn(weights[span, :], cot[span, :])
    small_dk[...] = (dk_s[...] * SCALE).astype(jnp.bfloat16)
    small_dv[...] = dv_s[...].astype(jnp.bfloat16)


def sum_over_mp(score):
    members = lax.axis_size("mp")
    step = 1
    while step < members:
        score = score + lax.ppermute(score, "mp", [(i, i ^ step) for i in range(members)])
        step *= 2
    return score


def number(x, z, c):
    return (x % X * Z + z % Z) * 2 + c % 2


def fetch(score, distance):
    pairs = []
    for x in range(X):
        for z in range(Z):
            for c in range(2):
                dx, dz, dc = distance(x, z, c)
                pairs.append((number(x + dx, z + dz, c + dc), number(x, z, c)))
    return lax.ppermute(score, "dp", pairs)


def gather_core(score):
    other = fetch(score, lambda x, z, c: (0, 0, 1))
    return jnp.concatenate([score, other, jnp.zeros((6, LANES), score.dtype)])


def gather_z(rows):
    return jnp.concatenate(
        [fetch(rows[0:2], lambda x, z, c: (0, step + 3 * c, 0)) for step in (1, 2, 3, 4)]
    )


def gathered_row(device, dev):
    my_c, my_z, my_x = dev & 1, (dev >> 1) & (Z - 1), dev >> 4
    c, z, x = device & 1, (device >> 1) & (Z - 1), device >> 4
    dx, dz = (x - my_x) & (X - 1), (z - my_z) & (Z - 1)
    fetcher = jnp.where(dz > 4, 1, 0)
    block = jnp.where(fetcher == my_c, 8, 16)
    fetched = block + 2 * (dz - 1 - 3 * fetcher) + (c ^ fetcher)
    row = jnp.where(dz == 0, c ^ my_c, fetched)
    return ((dx & 1) * 2 + (dx >> 1)) * 24 + row


def by_head(rows):
    return pl.BlockSpec((rows, HD), lambda h, *_: (0, h))


def whole(shape):
    return pl.BlockSpec(shape, lambda h, *_: (0, 0))


def image_spec(small_rows):
    return pl.BlockSpec((8, small_rows), lambda h, d, *_: (d[0] // 8, 0))


PARAMS = pltpu.CompilerParams(
    dimension_semantics=("arbitrary",), vmem_limit_bytes=60 * 2**20
)


def score_call(
    dev, counts, big_q, big_k, big_v, small_q, small_k, small_v, small_image, weight
):
    big_rows, features = big_q.shape
    small_rows = small_q.shape[0]
    return pl.pallas_call(
        score_kernel,
        grid_spec=pltpu.PrefetchScalarGridSpec(
            num_scalar_prefetch=2,
            grid=(1,),
            in_specs=[whole(big_q.shape)] * 3
            + [whole(small_q.shape)] * 3
            + [image_spec(small_rows), whole(weight.shape)],
            out_specs=whole((1, LANES)),
        ),
        out_shape=jax.ShapeDtypeStruct((1, LANES), jnp.float32),
        compiler_params=PARAMS,
        cost_estimate=pl.CostEstimate(
            flops=6 * 64 * (small_rows + big_rows) * features,
            bytes_accessed=6 * features * (big_rows + small_rows),
            transcendentals=64 * 5 * (small_rows + big_rows),
        ),
    )(dev, counts, big_q, big_k, big_v, small_q, small_k, small_v, small_image, weight)


def small_call(dev, small_q, small_k, small_v, small_image, owner, slot_rows):
    small_rows, features = small_q.shape
    heads = features // HD
    return pl.pallas_call(
        small_kernel,
        grid_spec=pltpu.PrefetchScalarGridSpec(
            num_scalar_prefetch=1,
            grid=(1,),
            in_specs=[whole(small_q.shape)] * 3 + [image_spec(small_rows), whole(owner.shape)],
            out_specs=whole((slot_rows, features)),
        ),
        out_shape=jax.ShapeDtypeStruct((slot_rows, features), jnp.bfloat16),
        compiler_params=PARAMS,
        cost_estimate=pl.CostEstimate(
            flops=2 * slot_rows * small_rows * features + 4 * small_rows * WINDOW * features,
            bytes_accessed=2 * features * (3 * small_rows + slot_rows),
            transcendentals=heads * small_rows * WINDOW,
        ),
    )(dev, small_q, small_k, small_v, small_image, owner)


def backward_call(
    dev, counts, big_q, big_k, big_v, big_dout, small_q, small_k, small_v, returned,
    small_image, owner, weight, near, far, pairs,
):
    big_rows, features = big_q.shape
    small_rows = small_q.shape[0]
    slot_rows = returned.shape[0]
    heads = features // HD
    pair_count = pairs.shape[1]
    bf16 = jnp.bfloat16
    return pl.pallas_call(
        backward_kernel,
        grid_spec=pltpu.PrefetchScalarGridSpec(
            num_scalar_prefetch=2,
            grid=(heads,),
            in_specs=[by_head(big_rows)] * 4
            + [by_head(small_rows)] * 3
            + [by_head(slot_rows)]
            + [image_spec(small_rows), whole(owner.shape), by_head(1)]
            + [whole(near.shape), whole(far.shape), whole(pairs.shape)],
            out_specs=[by_head(big_rows)] * 4
            + [by_head(small_rows)] * 3
            + [whole((1, pair_count))],
            scratch_shapes=[
                pltpu.VMEM((8, small_rows), jnp.int32),
                pltpu.VMEM((small_rows, LANES), jnp.float32),
                pltpu.VMEM((small_rows, slot_rows), bf16),
                pltpu.VMEM((big_rows, LANES), jnp.float32),
                pltpu.VMEM((small_rows, LANES), jnp.float32),
                pltpu.VMEM((small_rows, HD), jnp.float32),
                pltpu.VMEM((small_rows, HD), jnp.float32),
            ],
        ),
        out_shape=[jax.ShapeDtypeStruct((big_rows, features), bf16)] * 4
        + [jax.ShapeDtypeStruct((small_rows, features), bf16)] * 3
        + [jax.ShapeDtypeStruct((1, pair_count), jnp.float32)],
        compiler_params=PARAMS,
        cost_estimate=pl.CostEstimate(
            flops=12 * big_rows * big_rows * features + 10 * small_rows * WINDOW * features,
            bytes_accessed=2 * features * (8 * big_rows + 6 * small_rows + slot_rows),
            transcendentals=heads * (big_rows * big_rows + small_rows * WINDOW),
        ),
    )(
        dev, counts, big_q, big_k, big_v, big_dout, small_q, small_k, small_v, returned,
        small_image, owner, weight, near, far, pairs,
    )


def on_device(
    big_q, big_k, big_v, big_dout, big_counts, small_q, small_k, small_v,
    small_image, owner, owner_dout, reward_w, pair_perm,
):
    dev = lax.axis_index("dp").astype(jnp.int32).reshape(1)
    counts = big_counts.reshape(-1)
    weight = reward_w.reshape(1, -1)
    pairs = pair_perm.reshape(-1, 2).T
    returned = lax.all_to_all(owner_dout, "dp", split_axis=0, concat_axis=0, tiled=True)
    owner = owner.reshape(-1, LANES)
    score = score_call(
        dev, counts, big_q, big_k, big_v, small_q, small_k, small_v, small_image, weight
    )
    slots = small_call(
        dev, small_q, small_k, small_v, small_image, owner, owner_dout.shape[0]
    )
    near = gather_core(sum_over_mp(score))
    fetched = gather_z(near)
    slots, fetched, returned, pairs = lax.optimization_barrier((slots, fetched, returned, pairs))
    near = jnp.concatenate([near, fetched, fetch(fetched, lambda x, z, c: (0, 0, 1))])
    slots, near = lax.optimization_barrier((slots, near))
    small_out = lax.all_to_all(slots, "dp", split_axis=0, concat_axis=0, tiled=True)
    near = jnp.concatenate([near, fetch(near, lambda x, z, c: (2, 0, 0))])
    far = fetch(near, lambda x, z, c: (1, 0, 0))
    big_out, big_dq, big_dk, big_dv, small_dq, small_dk, small_dv, loss = backward_call(
        dev, counts, big_q, big_k, big_v, big_dout, small_q, small_k, small_v, returned,
        small_image, owner, weight, near, far, pairs,
    )
    small_out, loss = lax.optimization_barrier((small_out, loss.reshape(-1)))
    return (
        big_out, small_out, big_dq, big_dk, big_dv, small_dq, small_dk, small_dv,
        loss,
    )


def solution(mesh):
    rows = P("dp", "mp")
    return jax.shard_map(
        on_device,
        mesh=mesh,
        in_specs=(
            rows, rows, rows, rows, P("dp", None), rows, rows, rows, P(), P(), rows,
            P("mp"), P(),
        ),
        out_specs=(rows, rows, rows, rows, rows, rows, rows, rows, P()),
        check_vma=False,
    )
```

time: 146 us -> 91.4 us (0.63)
  the two profiles are of different devices: /device:TPU:6 before, /device:TPU:1 now
where the time goes in v2:
time: 91.4 us; the launch traced here: 91 us
  starting transfers between devices  39.3 us (43%)
  Pallas kernels  31 us (34%)
  waiting for transfers between devices  14.1 us (15%)
  local copies, waits for them, and re-layouts  3.98 us (4%)
  other arithmetic  1.99 us (2%)
    pallas_call x1, Pallas kernels, backward_call(): pl.pallas_call(backward_kernel, grid_spec=pltpu.PrefetchScalarGridSpec(nu...  20.5 us
    ppermute x8, starting transfers between devices, fetch(): return lax.ppermute(score, 'dp', pairs)  15.9 us
    all_to_all x1, starting transfers between devices, on_device(): lax.all_to_all(owner_dout, 'dp', split_axis=0, concat_axis=0, tiled=True)  13 us
    ppermute x8, waiting for transfers between devices, fetch(): return lax.ppermute(score, 'dp', pairs)  8.84 us
    all_to_all x1, starting transfers between devices, on_device(): lax.all_to_all(slots, 'dp', split_axis=0, concat_axis=0, tiled=True)  6.14 us
    pallas_call x1, Pallas kernels, small_call(): pl.pallas_call(small_kernel, grid_spec=pltpu.PrefetchScalarGridSpec(num_s...  5.9 us
    pallas_call x1, Pallas kernels, score_call(): pl.pallas_call(score_kernel, grid_spec=pltpu.PrefetchScalarGridSpec(num_s...  4.64 us
    ppermute x2, starting transfers between devices, sum_over_mp(): lax.ppermute(score, 'mp', [(i, i ^ step) for i in range(members)])  4.21 us
  transfers between devices with their start and end apart: 12, of which 9 were waited for; matrix products, arithmetic and copies ran while one was open for 5% of the time, Pallas kernels for 34%

profile of v2, /device:TPU:1, one launch (start us, length us, event | category | flops | bytes accessed | tf_op | source)
XLA Modules:
  0.0 91.0 jit_solution(2044433125010118056)
XLA Ops:
  0.7 13.0 %all-to-all-start = ((bf16[64,16,640]{2,1,0:T(8,128)(2,1)}), bf16[64,16,640]{2,1,0:T(8,128)(2,1)S(1)}, u32[]{:S(2)}, u32[]{:S(2)}) async-start(bf16[64,16,640]{2,1,0:T(8,128)(2,1)} %bitcast.9), calls=%async_computation | async-start | bytes 2621440 | tf_op jit(solution)/shard_map/all_to_all | solution.py:501
  13.7 0.6 reshape.43.w_ref
  14.3 4.6 %shard_map.197 = f32[1,128]{1,0:T(1,128)} custom-call(s32[1]{0:T(128)} %bitcast.dev_ref, s32[4]{0:T(128)} %bitcast.13, bf16[640,640]{1,0:T(8,128)(2,1)} %bq.3, bf16[640,640]{1,0:T(8,128)(2,1)} %bk.3, bf16[640,640]{1,0:T(8,128)(2,1)} %bv.3, bf16[512,640]{1,0:T(8,128)(2,1)} %sq.5, bf16[512,640]{1,0:T(8,128)(2,1)} %sk.5, bf16[512,640]{1,0:T(8,128)(2,1)} %sv.5, ...), custom_call_target="tpu_custom_call" | custom-call | flops 283115520 | bytes 4423680 | tf_op jit(solution)/shard_map/pallas_call | solution.py:404
  18.9 1.3 %collective-permute-start = (f32[1,128]{1,0:T(1,128)}, f32[1,128]{1,0:T(1,128)S(1)}, u32[]{:S(2)}, u32[]{:S(2)}) collective-permute-start(f32[1,128]{1,0:T(1,128)} %shard_map.197), channel_id=1, source_target_pairs={{0,1},{1,0},{2,3},{3,2},{4,5},{5,4},{6,7},{7,6},{8,9},{9,8},{10,11... | collective-permute-start | bytes 1544 | tf_op jit(solution)/shard_map/ppermute | solution.py:341
  20.2 1.5 %collective-permute-done = f32[1,128]{1,0:T(1,128)S(1)} collective-permute-done((f32[1,128]{1,0:T(1,128)}, f32[1,128]{1,0:T(1,128)S(1)}, u32[]{:S(2)}, u32[]{:S(2)}) %collective-permute-start) | collective-permute-done | bytes 544 | tf_op jit(solution)/shard_map/ppermute | solution.py:341
  21.7 0.7 add.6
  22.4 2.9 %collective-permute-start.1 = (f32[1,128]{1,0:T(1,128)S(1)}, f32[1,128]{1,0:T(1,128)S(1)}, u32[]{:S(2)}, u32[]{:S(2)}) collective-permute-start(f32[1,128]{1,0:T(1,128)S(1)} %add.6), channel_id=1, source_target_pairs={{0,2},{1,3},{2,0},{3,1},{4,6},{5,7},{6,4},{7,5},{8,10},{9,11},{10,... | collective-permute-start | bytes 1544 | tf_op jit(solution)/shard_map/ppermute | solution.py:341
  25.3 1.3 %collective-permute-done.1 = f32[1,128]{1,0:T(1,128)S(1)} collective-permute-done((f32[1,128]{1,0:T(1,128)S(1)}, f32[1,128]{1,0:T(1,128)S(1)}, u32[]{:S(2)}, u32[]{:S(2)}) %collective-permute-start.1) | collective-permute-done | bytes 544 | tf_op jit(solution)/shard_map/ppermute | solution.py:341
  26.6 2.2 %collective-permute-start.2 = (f32[1,128]{1,0:T(1,128)S(1)}, f32[1,128]{1,0:T(1,128)S(1)}, u32[]{:S(2)}, u32[]{:S(2)}) collective-permute-start(f32[1,128]{1,0:T(1,128)S(1)} %add.7), channel_id=1, source_target_pairs={{4,0},{0,4},{12,8},{8,12},{20,16},{16,20},{28,24},{24,28},{36,32},... | collective-permute-start | bytes 1544 | tf_op jit(solution)/shard_map/ppermute | solution.py:357
  28.7 0.8 collective-permute-done.2
  29.6 1.3 %collective-permute-start.6 = (f32[2,128]{1,0:T(2,128)S(1)}, f32[2,128]{1,0:T(2,128)S(1)}, u32[]{:S(2)}, u32[]{:S(2)}) collective-permute-start(f32[2,128]{1,0:T(2,128)S(1)} %pad_maximum_fusion.1), channel_id=1, source_target_pairs={{32,0},{60,4},{40,8},{4,12},{48,16},{12,20},{56,24},{20,28},{0,32}... | collective-permute-start | bytes 3080 | tf_op jit(solution)/shard_map/ppermute | solution.py:357
  30.8 2.1 %collective-permute-start.5 = (f32[2,128]{1,0:T(2,128)S(1)}, f32[2,128]{1,0:T(2,128)S(1)}, u32[]{:S(2)}, u32[]{:S(2)}) collective-permute-start(f32[2,128]{1,0:T(2,128)S(1)} %pad_maximum_fusion.1), channel_id=1, source_target_pairs={{24,0},{52,4},{32,8},{60,12},{40,16},{4,20},{48,24},{12,28},{56,32... | collective-permute-start | bytes 3080 | tf_op jit(solution)/shard_map/ppermute | solution.py:357
  32.9 2.4 %collective-permute-start.4 = (f32[2,128]{1,0:T(2,128)S(1)}, f32[2,128]{1,0:T(2,128)S(1)}, u32[]{:S(2)}, u32[]{:S(2)}) collective-permute-start(f32[2,128]{1,0:T(2,128)S(1)} %pad_maximum_fusion.1), channel_id=1, source_target_pairs={{16,0},{44,4},{24,8},{52,12},{32,16},{60,20},{40,24},{4,28},{48,32... | collective-permute-start | bytes 3080 | tf_op jit(solution)/shard_map/ppermute | solution.py:357
  35.3 2.1 %collective-permute-start.3 = (f32[2,128]{1,0:T(2,128)S(1)}, f32[2,128]{1,0:T(2,128)S(1)}, u32[]{:S(2)}, u32[]{:S(2)}) collective-permute-start(f32[2,128]{1,0:T(2,128)S(1)} %pad_maximum_fusion.1), channel_id=1, source_target_pairs={{8,0},{36,4},{16,8},{44,12},{24,16},{52,20},{32,24},{60,28},{40,32... | collective-permute-start | bytes 3080 | tf_op jit(solution)/shard_map/ppermute | solution.py:357
  37.4 5.9 %shard_map.196 = bf16[1024,640]{1,0:T(8,128)(2,1)} custom-call(s32[1]{0:T(128)} %bitcast.dev_ref, bf16[512,640]{1,0:T(8,128)(2,1)} %sq.5, bf16[512,640]{1,0:T(8,128)(2,1)} %sk.5, bf16[512,640]{1,0:T(8,128)(2,1)} %sv.5, s32[64,512]{1,0:T(8,128)} %image_ref.5, s32[24,128]{1,0:T(8,128)} %bitcast.15), custom_call_target="tpu_custom_call" | custom-call | flops 1006632960 | bytes 3276800 | tf_op jit(solution)/shard_map/pallas_call | solution.py:427
  43.3 0.8 reshape.44
  44.1 0.9 copy.22
  45.0 0.0 collective-permute-done.4
  45.0 2.8 %collective-permute-done.3 = f32[2,128]{1,0:T(2,128)S(1)} collective-permute-done((f32[2,128]{1,0:T(2,128)S(1)}, f32[2,128]{1,0:T(2,128)S(1)}, u32[]{:S(2)}, u32[]{:S(2)}) %collective-permute-start.3) | collective-permute-done | bytes 1056 | tf_op jit(solution)/shard_map/ppermute | solution.py:357
  47.9 0.1 all-to-all-done
  47.9 0.8 collective-permute-start.7
  48.8 0.8 collective-permute-done.7
  49.6 6.1 %all-to-all-start.1 = ((bf16[64,16,640]{2,1,0:T(8,128)(2,1)}), bf16[64,16,640]{2,1,0:T(8,128)(2,1)S(1)}, u32[]{:S(2)}, u32[]{:S(2)}) async-start(bf16[64,16,640]{2,1,0:T(8,128)(2,1)} %bitcast.11), calls=%async_computation.1 | async-start | bytes 2621440 | tf_op jit(solution)/shard_map/all_to_all | solution.py:514
  55.8 3.3 %collective-permute-start.8 = (f32[24,128]{1,0:T(8,128)S(1)}, f32[24,128]{1,0:T(8,128)S(1)}, u32[]{:S(2)}, u32[]{:S(2)}) collective-permute-start(f32[24,128]{1,0:T(8,128)S(1)} %concatenate.16), channel_id=1, source_target_pairs={{128,0},{132,4},{136,8},{140,12},{144,16},{148,20},{152,24},{156,2... | collective-permute-start | bytes 36872 | tf_op jit(solution)/shard_map/ppermute | solution.py:357
  59.0 2.8 %collective-permute-done.8 = f32[24,128]{1,0:T(8,128)S(1)} collective-permute-done((f32[24,128]{1,0:T(8,128)S(1)}, f32[24,128]{1,0:T(8,128)S(1)}, u32[]{:S(2)}, u32[]{:S(2)}) %collective-permute-start.8) | collective-permute-done | bytes 12320 | tf_op jit(solution)/shard_map/ppermute | solution.py:357
  61.8 1.8 %collective-permute-start.9 = (f32[48,128]{1,0:T(8,128)S(1)}, f32[48,128]{1,0:T(8,128)S(1)}, u32[]{:S(2)}, u32[]{:S(2)}) collective-permute-start(f32[48,128]{1,0:T(8,128)S(1)} %constant_dynamic-update-slice_fusion.near_ref), channel_id=1, source_target_pairs={{64,0},{68,4},{72,8},{76,12},{80,16},{84,20},{88,24},{92,28},{96,3... | collective-permute-start | bytes 73736 | tf_op jit(solution)/shard_map/ppermute | solution.py:357
  63.6 1.6 %collective-permute-done.9.far_ref = f32[48,128]{1,0:T(8,128)S(1)} collective-permute-done((f32[48,128]{1,0:T(8,128)S(1)}, f32[48,128]{1,0:T(8,128)S(1)}, u32[]{:S(2)}, u32[]{:S(2)}) %collective-permute-start.9) | collective-permute-done | bytes 24608 | tf_op jit(solution)/shard_map/ppermute | solution.py:357
  65.2 0.6 copy-done.4
  65.8 20.5 %shard_map.198 = (bf16[640,640]{1,0:T(8,128)(2,1)}, bf16[640,640]{1,0:T(8,128)(2,1)}, bf16[640,640]{1,0:T(8,128)(2,1)}, bf16[640,640]{1,0:T(8,128)(2,1)}, bf16[5...) custom-call(s32[1]{0:T(128)} %bitcast.dev_ref, s32[4]{0:T(128)} %bitcast.14, ...), custom_call_target="tpu_custom_call" | custom-call | flops 3984588800 | bytes 11796480 | tf_op jit(solution)/shard_map/pallas_call | solution.py:455
  86.3 1.3 %reduce = f32[1664]{0:T(1024)} reduce(f32[1,1664]{1,0:T(1,128)} %get-tuple-element.32, f32[]{:T(128)} %constant.9), dimensions={0}, to_apply=%get-tuple-element.32.reduce_sub_computation | reduce | bytes 13316 | tf_op jit(solution)/shard_map/pallas_call | solution.py:455
  87.6 2.4 %all-to-all-done.1 = bf16[64,16,640]{2,1,0:T(8,128)(2,1)S(1)} async-done(((bf16[64,16,640]{2,1,0:T(8,128)(2,1)}), bf16[64,16,640]{2,1,0:T(8,128)(2,1)S(1)}, u32[]{:S(2)}, u32[]{:S(2)}) %all-to-all-start.1) | async-done | bytes 1310752 | tf_op jit(solution)/shard_map/all_to_all | solution.py:514
  89.9 1.1 %copy.25 = bf16[1024,640]{1,0:T(8,128)(2,1)} copy(bf16[1024,640]{1,0:T(8,128)(2,1)S(1)} %bitcast.8) | data formatting | bytes 2621440
  (18 shorter events, 0.1 us)
Async XLA Ops:
  0.6 13.0 %copy-start.3 = (f32[640]{0:T(1024)S(1)}, f32[640]{0:T(1024)}, u32[]{:S(2)}) copy-start(f32[640]{0:T(1024)} %param.24) | copy-start | bytes 7684
  0.7 47.3 %all-to-all-start = ((bf16[64,16,640]{2,1,0:T(8,128)(2,1)}), bf16[64,16,640]{2,1,0:T(8,128)(2,1)S(1)}, u32[]{:S(2)}, u32[]{:S(2)}) async-start(bf16[64,16,640]{2,1,0:T(8,128)(2,1)} %bitcast.9), calls=%async_computation | async-start | bytes 2621440 | tf_op jit(solution)/shard_map/all_to_all | solution.py:501
  18.9 2.8 %collective-permute-start = (f32[1,128]{1,0:T(1,128)}, f32[1,128]{1,0:T(1,128)S(1)}, u32[]{:S(2)}, u32[]{:S(2)}) collective-permute-start(f32[1,128]{1,0:T(1,128)} %shard_map.197), channel_id=1, source_target_pairs={{0,1},{1,0},{2,3},{3,2},{4,5},{5,4},{6,7},{7,6},{8,9},{9,8},{10,11... | collective-permute-start | bytes 1544 | tf_op jit(solution)/shard_map/ppermute | solution.py:341
  22.4 4.2 %collective-permute-start.1 = (f32[1,128]{1,0:T(1,128)S(1)}, f32[1,128]{1,0:T(1,128)S(1)}, u32[]{:S(2)}, u32[]{:S(2)}) collective-permute-start(f32[1,128]{1,0:T(1,128)S(1)} %add.6), channel_id=1, source_target_pairs={{0,2},{1,3},{2,0},{3,1},{4,6},{5,7},{6,4},{7,5},{8,10},{9,11},{10,... | collective-permute-start | bytes 1544 | tf_op jit(solution)/shard_map/ppermute | solution.py:341
  26.6 3.0 %collective-permute-start.2 = (f32[1,128]{1,0:T(1,128)S(1)}, f32[1,128]{1,0:T(1,128)S(1)}, u32[]{:S(2)}, u32[]{:S(2)}) collective-permute-start(f32[1,128]{1,0:T(1,128)S(1)} %add.7), channel_id=1, source_target_pairs={{4,0},{0,4},{12,8},{8,12},{20,16},{16,20},{28,24},{24,28},{36,32},... | collective-permute-start | bytes 1544 | tf_op jit(solution)/shard_map/ppermute | solution.py:357
  29.6 15.5 %collective-permute-start.6 = (f32[2,128]{1,0:T(2,128)S(1)}, f32[2,128]{1,0:T(2,128)S(1)}, u32[]{:S(2)}, u32[]{:S(2)}) collective-permute-start(f32[2,128]{1,0:T(2,128)S(1)} %pad_maximum_fusion.1), channel_id=1, source_target_pairs={{32,0},{60,4},{40,8},{4,12},{48,16},{12,20},{56,24},{20,28},{0,32}... | collective-permute-start | bytes 3080 | tf_op jit(solution)/shard_map/ppermute | solution.py:357
  30.8 14.2 %collective-permute-start.5 = (f32[2,128]{1,0:T(2,128)S(1)}, f32[2,128]{1,0:T(2,128)S(1)}, u32[]{:S(2)}, u32[]{:S(2)}) collective-permute-start(f32[2,128]{1,0:T(2,128)S(1)} %pad_maximum_fusion.1), channel_id=1, source_target_pairs={{24,0},{52,4},{32,8},{60,12},{40,16},{4,20},{48,24},{12,28},{56,32... | collective-permute-start | bytes 3080 | tf_op jit(solution)/shard_map/ppermute | solution.py:357
  32.9 12.1 %collective-permute-start.4 = (f32[2,128]{1,0:T(2,128)S(1)}, f32[2,128]{1,0:T(2,128)S(1)}, u32[]{:S(2)}, u32[]{:S(2)}) collective-permute-start(f32[2,128]{1,0:T(2,128)S(1)} %pad_maximum_fusion.1), channel_id=1, source_target_pairs={{16,0},{44,4},{24,8},{52,12},{32,16},{60,20},{40,24},{4,28},{48,32... | collective-permute-start | bytes 3080 | tf_op jit(solution)/shard_map/ppermute | solution.py:357
  35.3 12.5 %collective-permute-start.3 = (f32[2,128]{1,0:T(2,128)S(1)}, f32[2,128]{1,0:T(2,128)S(1)}, u32[]{:S(2)}, u32[]{:S(2)}) collective-permute-start(f32[2,128]{1,0:T(2,128)S(1)} %pad_maximum_fusion.1), channel_id=1, source_target_pairs={{8,0},{36,4},{16,8},{44,12},{24,16},{52,20},{32,24},{60,28},{40,32... | collective-permute-start | bytes 3080 | tf_op jit(solution)/shard_map/ppermute | solution.py:357
  37.4 5.9 %copy-start.1 = (s32[3328]{0:T(1024)S(1)}, s32[3328]{0:T(1024)}, u32[]{:S(2)}) copy-start(s32[3328]{0:T(1024)} %param.25) | copy-start | bytes 39940
  47.9 1.7 %copy-start = (bf16[64,16,640]{2,1,0:T(8,128)(2,1)}, bf16[64,16,640]{2,1,0:T(8,128)(2,1)S(1)}, u32[]{:S(2)}) copy-start(bf16[64,16,640]{2,1,0:T(8,128)(2,1)S(1)} %all-to-all-done) | copy-start | bytes 3932164
  47.9 1.7 %collective-permute-start.7 = (f32[8,128]{1,0:T(8,128)S(1)}, f32[8,128]{1,0:T(8,128)S(1)}, u32[]{:S(2)}, u32[]{:S(2)}) collective-permute-start(f32[8,128]{1,0:T(8,128)S(1)} %pad_maximum_fusion), channel_id=1, source_target_pairs={{4,0},{0,4},{12,8},{8,12},{20,16},{16,20},{28,24},{24,28},{36,32},... | collective-permute-start | bytes 12296 | tf_op jit(solution)/shard_map/ppermute | solution.py:357
  49.6 40.3 %all-to-all-start.1 = ((bf16[64,16,640]{2,1,0:T(8,128)(2,1)}), bf16[64,16,640]{2,1,0:T(8,128)(2,1)S(1)}, u32[]{:S(2)}, u32[]{:S(2)}) async-start(bf16[64,16,640]{2,1,0:T(8,128)(2,1)} %bitcast.11), calls=%async_computation.1 | async-start | bytes 2621440 | tf_op jit(solution)/shard_map/all_to_all | solution.py:514
  55.8 6.0 %collective-permute-start.8 = (f32[24,128]{1,0:T(8,128)S(1)}, f32[24,128]{1,0:T(8,128)S(1)}, u32[]{:S(2)}, u32[]{:S(2)}) collective-permute-start(f32[24,128]{1,0:T(8,128)S(1)} %concatenate.16), channel_id=1, source_target_pairs={{128,0},{132,4},{136,8},{140,12},{144,16},{148,20},{152,24},{156,2... | collective-permute-start | bytes 36872 | tf_op jit(solution)/shard_map/ppermute | solution.py:357
  61.8 3.4 %copy-start.2 = (f32[48,128]{1,0:T(8,128)}, f32[48,128]{1,0:T(8,128)S(1)}, u32[]{:S(2)}) copy-start(f32[48,128]{1,0:T(8,128)S(1)} %constant_dynamic-update-slice_fusion.near_ref) | copy-start | bytes 73732
  61.8 3.4 %collective-permute-start.9 = (f32[48,128]{1,0:T(8,128)S(1)}, f32[48,128]{1,0:T(8,128)S(1)}, u32[]{:S(2)}, u32[]{:S(2)}) collective-permute-start(f32[48,128]{1,0:T(8,128)S(1)} %constant_dynamic-update-slice_fusion.near_ref), channel_id=1, source_target_pairs={{64,0},{68,4},{72,8},{76,12},{80,16},{84,20},{88,24},{92,28},{96,3... | collective-permute-start | bytes 73736 | tf_op jit(solution)/shard_map/ppermute | solution.py:357
  65.2 0.6 copy-start.4

commit v3 on v2

--- a/solution.py
+++ b/solution.py
@@ -277,26 +277,50 @@
         first_small = X * Z * 2 * BIG_IMG
         table = jnp.concatenate([near_ref[...], far_ref[...]])
         table = jnp.transpose(table)[0:56, :]
-        preferred = pairs_ref[0:1, :]
-        rejected = pairs_ref[1:2, :]
-        margin = pick(table, rejected, first_small, dev) - pick(
-            table, preferred, first_small, dev
-        )
+        images = pairs_ref[...]
+        lines = images.shape[0]
+        flat = jnp.concatenate([images[r : r + 1, :] for r in range(lines)], axis=1)
+        scores = pick(table, flat, first_small, dev)
+        scores = jnp.concatenate(
+            [scores[:, r * LANES : (r + 1) * LANES] for r in range(lines)], axis=0
+        )
+        rejected = (iota(scores.shape, 1) & 1) == 1
+        after = pltpu.roll(scores, LANES - 1, 1)
+        before = pltpu.roll(scores, 1, 1)
+        margin = jnp.where(rejected, scores - before, after - scores)
         small_exp = jnp.exp(-jnp.abs(margin))
-        loss_out[...] = jnp.maximum(margin, 0.0) + jnp.log1p(small_exp)
+        loss = jnp.maximum(margin, 0.0) + jnp.log1p(small_exp)
         pull = jnp.where(margin >= 0, 1.0, small_exp) / (1.0 + small_exp)
-        lane = iota((LANES, 1), 0)
+        signed = jnp.where(rejected, pull, -pull)
+        source, target = iota((LANES, LANES), 0), iota((LANES, LANES), 1)
+        half = LANES // 2
+
+        def squeezed(offset):
+            chosen = (source == 2 * (target - offset)) & (target >= offset)
+            chosen = chosen & (target < offset + half)
+            return jnp.dot(
+                loss,
+                chosen.astype(jnp.float32),
+                preferred_element_type=jnp.float32,
+                precision=lax.Precision.HIGHEST,
+            )
+
+        left, right = squeezed(0), squeezed(half)
+        loss_out[...] = jnp.concatenate(
+            [left[r : r + 1, :] + right[r + 1 : r + 2, :] for r in range(0, lines, 2)],
+            axis=1,
+        ).reshape(-1)
+        lane = iota((64, 1), 0)
         number = jnp.where(
             lane < BIG_IMG,
             dev * BIG_IMG + lane,
             jnp.where(lane < IMAGES, first_small + dev * MIG_IMG + lane - BIG_IMG, -1),
         )
-        gain = jnp.sum(
-            jnp.where(rejected == number, pull, 0.0)
-            - jnp.where(preferred == number, pull, 0.0),
-            axis=1,
-            keepdims=True,
-        )
+        gain = jnp.zeros((64, LANES), jnp.float32)
+        for r in range(lines):
+            gain = gain + jnp.where(images[r : r + 1, :] == number, signed[r : r + 1, :], 0.0)
+        gain = jnp.sum(gain, axis=1, keepdims=True)
+        gain = jnp.concatenate([gain, jnp.zeros_like(gain)], axis=0)
         gain_row = jnp.transpose(jnp.broadcast_to(gain, (LANES, LANES)))[0:1, :]
         big_gain_s[...] = jnp.broadcast_to(
             jnp.sum(class_mask_big(big_rows, counts_ref) * gain_row, axis=1, keepdims=True),
@@ -391,9 +415,10 @@
     return pl.BlockSpec((8, small_rows), lambda h, d, *_: (d[0] // 8, 0))
 
 
-PARAMS = pltpu.CompilerParams(
-    dimension_semantics=("arbitrary",), vmem_limit_bytes=60 * 2**20
-)
+def params(mebibytes):
+    return pltpu.CompilerParams(
+        dimension_semantics=("arbitrary",), vmem_limit_bytes=mebibytes * 2**20
+    )
 
 
 def score_call(
@@ -412,7 +437,7 @@
             out_specs=whole((1, LANES)),
         ),
         out_shape=jax.ShapeDtypeStruct((1, LANES), jnp.float32),
-        compiler_params=PARAMS,
+        compiler_params=params(63),
         cost_estimate=pl.CostEstimate(
             flops=6 * 64 * (small_rows + big_rows) * features,
             bytes_accessed=6 * features * (big_rows + small_rows),
@@ -433,7 +458,7 @@
             out_specs=whole((slot_rows, features)),
         ),
         out_shape=jax.ShapeDtypeStruct((slot_rows, features), jnp.bfloat16),
-        compiler_params=PARAMS,
+        compiler_params=params(63),
         cost_estimate=pl.CostEstimate(
             flops=2 * slot_rows * small_rows * features + 4 * small_rows * WINDOW * features,
             bytes_accessed=2 * features * (3 * small_rows + slot_rows),
@@ -450,7 +475,7 @@
     small_rows = small_q.shape[0]
     slot_rows = returned.shape[0]
     heads = features // HD
-    pair_count = pairs.shape[1]
+    pair_count = pairs.size // 2
     bf16 = jnp.bfloat16
     return pl.pallas_call(
         backward_kernel,
@@ -464,7 +489,7 @@
             + [whole(near.shape), whole(far.shape), whole(pairs.shape)],
             out_specs=[by_head(big_rows)] * 4
             + [by_head(small_rows)] * 3
-            + [whole((1, pair_count))],
+            + [pl.BlockSpec((pair_count,), lambda h, *_: (0,))],
             scratch_shapes=[
                 pltpu.VMEM((8, small_rows), jnp.int32),
                 pltpu.VMEM((small_rows, LANES), jnp.float32),
@@ -477,8 +502,8 @@
         ),
         out_shape=[jax.ShapeDtypeStruct((big_rows, features), bf16)] * 4
         + [jax.ShapeDtypeStruct((small_rows, features), bf16)] * 3
-        + [jax.ShapeDtypeStruct((1, pair_count), jnp.float32)],
-        compiler_params=PARAMS,
+        + [jax.ShapeDtypeStruct((pair_count,), jnp.float32)],
+        compiler_params=params(60),
         cost_estimate=pl.CostEstimate(
             flops=12 * big_rows * big_rows * features + 10 * small_rows * WINDOW * features,
             bytes_accessed=2 * features * (8 * big_rows + 6 * small_rows + slot_rows),
@@ -497,7 +522,7 @@
     dev = lax.axis_index("dp").astype(jnp.int32).reshape(1)
     counts = big_counts.reshape(-1)
     weight = reward_w.reshape(1, -1)
-    pairs = pair_perm.reshape(-1, 2).T
+    pairs = pair_perm.reshape(-1, LANES)
     returned = lax.all_to_all(owner_dout, "dp", split_axis=0, concat_axis=0, tiled=True)
     owner = owner.reshape(-1, LANES)
     score = score_call(
@@ -508,17 +533,16 @@
     )
     near = gather_core(sum_over_mp(score))
     fetched = gather_z(near)
-    slots, fetched, returned, pairs = lax.optimization_barrier((slots, fetched, returned, pairs))
+    slots, fetched, returned = lax.optimization_barrier((slots, fetched, returned))
+    small_out = lax.all_to_all(slots, "dp", split_axis=0, concat_axis=0, tiled=True)
     near = jnp.concatenate([near, fetched, fetch(fetched, lambda x, z, c: (0, 0, 1))])
-    slots, near = lax.optimization_barrier((slots, near))
-    small_out = lax.all_to_all(slots, "dp", split_axis=0, concat_axis=0, tiled=True)
     near = jnp.concatenate([near, fetch(near, lambda x, z, c: (2, 0, 0))])
     far = fetch(near, lambda x, z, c: (1, 0, 0))
     big_out, big_dq, big_dk, big_dv, small_dq, small_dk, small_dv, loss = backward_call(
         dev, counts, big_q, big_k, big_v, big_dout, small_q, small_k, small_v, returned,
         small_image, owner, weight, near, far, pairs,
     )
-    small_out, loss = lax.optimization_barrier((small_out, loss.reshape(-1)))
+    small_out, loss = lax.optimization_barrier((small_out, loss))
     return (
         big_out, small_out, big_dq, big_dk, big_dv, small_dq, small_dk, small_dv,
         loss,

time: 91.4 us -> 89.8 us (0.982)
  local copies, waits for them, and re-layouts: 3.98 us -> 2.3 us
  other arithmetic: 1.99 us -> 0.68 us
    reshape x2 -> x0, local copies, waits for them, and re-layouts: 1.69 us -> none  [on_device(): pairs = pair_perm.reshape(-1, 2).T]
    pallas_call x1 -> x0, other arithmetic: 1.31 us -> none  [backward_call(): pl.pallas_call(backward_kernel, grid_spec=pltpu.PrefetchScalarGridSpec(nu...]
  transfers between devices with their start and end apart: 12 -> 12, of which waited for: 9 -> 10; matrix products, arithmetic and copies ran while one was open for 5% -> 1% of each run, Pallas kernels for 34% -> 35%
where the time goes in v3:
time: 89.8 us; the launch traced here: 89.4 us
  starting transfers between devices  39.8 us (44%)
  Pallas kernels  31 us (35%)
  waiting for transfers between devices  15 us (17%)
  local copies, waits for them, and re-layouts  2.3 us (3%)
    pallas_call x1, Pallas kernels, backward_call(): pl.pallas_call(backward_kernel, grid_spec=pltpu.PrefetchScalarGridSpec(nu...  20.5 us
    ppermute x8, starting transfers between devices, fetch(): return lax.ppermute(score, 'dp', pairs)  16.3 us
    all_to_all x1, starting transfers between devices, on_device(): lax.all_to_all(owner_dout, 'dp', split_axis=0, concat_axis=0, tiled=True)  13.2 us
    ppermute x8, waiting for transfers between devices, fetch(): return lax.ppermute(score, 'dp', pairs)  8.64 us
    all_to_all x1, starting transfers between devices, on_device(): lax.all_to_all(slots, 'dp', split_axis=0, concat_axis=0, tiled=True)  6.12 us
    pallas_call x1, Pallas kernels, small_call(): pl.pallas_call(small_kernel, grid_spec=pltpu.PrefetchScalarGridSpec(num_s...  5.86 us
    pallas_call x1, Pallas kernels, score_call(): pl.pallas_call(score_kernel, grid_spec=pltpu.PrefetchScalarGridSpec(num_s...  4.64 us
    ppermute x2, starting transfers between devices, sum_over_mp(): lax.ppermute(score, 'mp', [(i, i ^ step) for i in range(members)])  4.21 us
  transfers between devices with their start and end apart: 12, of which 10 were waited for; matrix products, arithmetic and copies ran while one was open for 1% of the time, Pallas kernels for 35%

profile of v3, /device:TPU:1, one launch (start us, length us, event | category | flops | bytes accessed | tf_op | source)
XLA Modules:
  0.0 89.4 jit_solution(17909681073174357942)
XLA Ops:
  0.6 0.0 copy-start.1
  0.7 13.2 %all-to-all-start = ((bf16[64,16,640]{2,1,0:T(8,128)(2,1)}), bf16[64,16,640]{2,1,0:T(8,128)(2,1)}, u32[]{:S(2)}, u32[]{:S(2)}) async-start(bf16[64,16,640]{2,1,0:T(8,128)(2,1)} %bitcast.9), calls=%async_computation | async-start | bytes 2621440 | tf_op jit(solution)/shard_map/all_to_all | solution.py:526
  13.8 0.6 reshape.40.w_ref
  14.4 4.6 %shard_map.197 = f32[1,128]{1,0:T(1,128)} custom-call(s32[1]{0:T(128)} %bitcast.dev_ref, s32[4]{0:T(128)} %bitcast.11, bf16[640,640]{1,0:T(8,128)(2,1)} %bq.3, bf16[640,640]{1,0:T(8,128)(2,1)} %bk.3, bf16[640,640]{1,0:T(8,128)(2,1)} %bv.3, bf16[512,640]{1,0:T(8,128)(2,1)} %sq.5, bf16[512,640]{1,0:T(8,128)(2,1)} %sk.5, bf16[512,640]{1,0:T(8,128)(2,1)} %sv.5, ...), custom_call_target="tpu_custom_call" | custom-call | flops 283115520 | bytes 4423680 | tf_op jit(solution)/shard_map/pallas_call | solution.py:429
  19.1 1.3 %collective-permute-start = (f32[1,128]{1,0:T(1,128)}, f32[1,128]{1,0:T(1,128)S(1)}, u32[]{:S(2)}, u32[]{:S(2)}) collective-permute-start(f32[1,128]{1,0:T(1,128)} %shard_map.197), channel_id=1, source_target_pairs={{0,1},{1,0},{2,3},{3,2},{4,5},{5,4},{6,7},{7,6},{8,9},{9,8},{10,11... | collective-permute-start | bytes 1544 | tf_op jit(solution)/shard_map/ppermute | solution.py:365
  20.4 1.6 %collective-permute-done = f32[1,128]{1,0:T(1,128)S(1)} collective-permute-done((f32[1,128]{1,0:T(1,128)}, f32[1,128]{1,0:T(1,128)S(1)}, u32[]{:S(2)}, u32[]{:S(2)}) %collective-permute-start) | collective-permute-done | bytes 544 | tf_op jit(solution)/shard_map/ppermute | solution.py:365
  22.0 0.7 add.6
  22.7 2.9 %collective-permute-start.1 = (f32[1,128]{1,0:T(1,128)S(1)}, f32[1,128]{1,0:T(1,128)S(1)}, u32[]{:S(2)}, u32[]{:S(2)}) collective-permute-start(f32[1,128]{1,0:T(1,128)S(1)} %add.6), channel_id=1, source_target_pairs={{0,2},{1,3},{2,0},{3,1},{4,6},{5,7},{6,4},{7,5},{8,10},{9,11},{10,... | collective-permute-start | bytes 1544 | tf_op jit(solution)/shard_map/ppermute | solution.py:365
  25.6 1.4 %collective-permute-done.1 = f32[1,128]{1,0:T(1,128)S(1)} collective-permute-done((f32[1,128]{1,0:T(1,128)S(1)}, f32[1,128]{1,0:T(1,128)S(1)}, u32[]{:S(2)}, u32[]{:S(2)}) %collective-permute-start.1) | collective-permute-done | bytes 544 | tf_op jit(solution)/shard_map/ppermute | solution.py:365
  27.0 2.0 %collective-permute-start.2 = (f32[1,128]{1,0:T(1,128)S(1)}, f32[1,128]{1,0:T(1,128)S(1)}, u32[]{:S(2)}, u32[]{:S(2)}) collective-permute-start(f32[1,128]{1,0:T(1,128)S(1)} %add.7), channel_id=1, source_target_pairs={{4,0},{0,4},{12,8},{8,12},{20,16},{16,20},{28,24},{24,28},{36,32},... | collective-permute-start | bytes 1544 | tf_op jit(solution)/shard_map/ppermute | solution.py:381
  29.0 0.8 collective-permute-done.2
  29.8 1.2 %collective-permute-start.6 = (f32[2,128]{1,0:T(2,128)S(1)}, f32[2,128]{1,0:T(2,128)S(1)}, u32[]{:S(2)}, u32[]{:S(2)}) collective-permute-start(f32[2,128]{1,0:T(2,128)S(1)} %pad_maximum_fusion.1), channel_id=1, source_target_pairs={{32,0},{60,4},{40,8},{4,12},{48,16},{12,20},{56,24},{20,28},{0,32}... | collective-permute-start | bytes 3080 | tf_op jit(solution)/shard_map/ppermute | solution.py:381
  31.0 2.1 %collective-permute-start.5 = (f32[2,128]{1,0:T(2,128)S(1)}, f32[2,128]{1,0:T(2,128)S(1)}, u32[]{:S(2)}, u32[]{:S(2)}) collective-permute-start(f32[2,128]{1,0:T(2,128)S(1)} %pad_maximum_fusion.1), channel_id=1, source_target_pairs={{24,0},{52,4},{32,8},{60,12},{40,16},{4,20},{48,24},{12,28},{56,32... | collective-permute-start | bytes 3080 | tf_op jit(solution)/shard_map/ppermute | solution.py:381
  33.1 2.4 %collective-permute-start.4 = (f32[2,128]{1,0:T(2,128)S(1)}, f32[2,128]{1,0:T(2,128)S(1)}, u32[]{:S(2)}, u32[]{:S(2)}) collective-permute-start(f32[2,128]{1,0:T(2,128)S(1)} %pad_maximum_fusion.1), channel_id=1, source_target_pairs={{16,0},{44,4},{24,8},{52,12},{32,16},{60,20},{40,24},{4,28},{48,32... | collective-permute-start | bytes 3080 | tf_op jit(solution)/shard_map/ppermute | solution.py:381
  35.5 2.1 %collective-permute-start.3 = (f32[2,128]{1,0:T(2,128)S(1)}, f32[2,128]{1,0:T(2,128)S(1)}, u32[]{:S(2)}, u32[]{:S(2)}) collective-permute-start(f32[2,128]{1,0:T(2,128)S(1)} %pad_maximum_fusion.1), channel_id=1, source_target_pairs={{8,0},{36,4},{16,8},{44,12},{24,16},{52,20},{32,24},{60,28},{40,32... | collective-permute-start | bytes 3080 | tf_op jit(solution)/shard_map/ppermute | solution.py:381
  37.6 5.9 %shard_map.196 = bf16[1024,640]{1,0:T(8,128)(2,1)} custom-call(s32[1]{0:T(128)} %bitcast.dev_ref, bf16[512,640]{1,0:T(8,128)(2,1)} %sq.5, bf16[512,640]{1,0:T(8,128)(2,1)} %sk.5, bf16[512,640]{1,0:T(8,128)(2,1)} %sv.5, s32[64,512]{1,0:T(8,128)} %image_ref.5, s32[24,128]{1,0:T(8,128)} %bitcast.14), custom_call_target="tpu_custom_call" | custom-call | flops 1006632960 | bytes 3276800 | tf_op jit(solution)/shard_map/pallas_call | solution.py:452
  43.5 0.0 collective-permute-done.6
  43.5 1.5 %collective-permute-done.5 = f32[2,128]{1,0:T(2,128)S(1)} collective-permute-done((f32[2,128]{1,0:T(2,128)S(1)}, f32[2,128]{1,0:T(2,128)S(1)}, u32[]{:S(2)}, u32[]{:S(2)}) %collective-permute-start.5) | collective-permute-done | bytes 1056 | tf_op jit(solution)/shard_map/ppermute | solution.py:381
  45.0 0.0 collective-permute-done.4
  45.0 2.9 %collective-permute-done.3 = f32[2,128]{1,0:T(2,128)S(1)} collective-permute-done((f32[2,128]{1,0:T(2,128)S(1)}, f32[2,128]{1,0:T(2,128)S(1)}, u32[]{:S(2)}, u32[]{:S(2)}) %collective-permute-start.3) | collective-permute-done | bytes 1056 | tf_op jit(solution)/shard_map/ppermute | solution.py:381
  47.9 0.2 all-to-all-done
  48.0 6.1 %all-to-all-start.1 = ((bf16[64,16,640]{2,1,0:T(8,128)(2,1)}), bf16[64,16,640]{2,1,0:T(8,128)(2,1)S(1)}, u32[]{:S(2)}, u32[]{:S(2)}) async-start(bf16[64,16,640]{2,1,0:T(8,128)(2,1)} %bitcast.10), calls=%async_computation.1 | async-start | bytes 2621440 | tf_op jit(solution)/shard_map/all_to_all | solution.py:537
  54.2 0.5 collective-permute-start.7
  54.7 0.8 collective-permute-done.7
  55.6 3.0 %collective-permute-start.8 = (f32[24,128]{1,0:T(8,128)S(1)}, f32[24,128]{1,0:T(8,128)S(1)}, u32[]{:S(2)}, u32[]{:S(2)}) collective-permute-start(f32[24,128]{1,0:T(8,128)S(1)} %concatenate.17), channel_id=1, source_target_pairs={{128,0},{132,4},{136,8},{140,12},{144,16},{148,20},{152,24},{156,2... | collective-permute-start | bytes 36872 | tf_op jit(solution)/shard_map/ppermute | solution.py:381
  58.5 1.6 %collective-permute-done.8 = f32[24,128]{1,0:T(8,128)S(1)} collective-permute-done((f32[24,128]{1,0:T(8,128)S(1)}, f32[24,128]{1,0:T(8,128)S(1)}, u32[]{:S(2)}, u32[]{:S(2)}) %collective-permute-start.8) | collective-permute-done | bytes 12320 | tf_op jit(solution)/shard_map/ppermute | solution.py:381
  60.2 3.0 %collective-permute-start.9 = (f32[48,128]{1,0:T(8,128)S(1)}, f32[48,128]{1,0:T(8,128)S(1)}, u32[]{:S(2)}, u32[]{:S(2)}) collective-permute-start(f32[48,128]{1,0:T(8,128)S(1)} %concatenate.18.near_ref), channel_id=1, source_target_pairs={{64,0},{68,4},{72,8},{76,12},{80,16},{84,20},{88,24},{92,28},{96,3... | collective-permute-start | bytes 73736 | tf_op jit(solution)/shard_map/ppermute | solution.py:381
  63.2 0.9 %collective-permute-done.9.far_ref = f32[48,128]{1,0:T(8,128)S(1)} collective-permute-done((f32[48,128]{1,0:T(8,128)S(1)}, f32[48,128]{1,0:T(8,128)S(1)}, u32[]{:S(2)}, u32[]{:S(2)}) %collective-permute-start.9) | collective-permute-done | bytes 24608 | tf_op jit(solution)/shard_map/ppermute | solution.py:381
  64.1 0.6 copy-done.2
  64.7 20.5 %shard_map.198 = (bf16[640,640]{1,0:T(8,128)(2,1)}, bf16[640,640]{1,0:T(8,128)(2,1)}, bf16[640,640]{1,0:T(8,128)(2,1)}, bf16[640,640]{1,0:T(8,128)(2,1)}, bf16[5...) custom-call(s32[1]{0:T(128)} %bitcast.dev_ref, s32[4]{0:T(128)} %bitcast.12, ...), custom_call_target="tpu_custom_call" | custom-call | flops 3984588800 | bytes 11796480 | tf_op jit(solution)/shard_map/pallas_call | solution.py:480
  85.2 3.1 %all-to-all-done.1 = bf16[64,16,640]{2,1,0:T(8,128)(2,1)S(1)} async-done(((bf16[64,16,640]{2,1,0:T(8,128)(2,1)}), bf16[64,16,640]{2,1,0:T(8,128)(2,1)S(1)}, u32[]{:S(2)}, u32[]{:S(2)}) %all-to-all-start.1) | async-done | bytes 1310752 | tf_op jit(solution)/shard_map/all_to_all | solution.py:537
  88.3 1.1 %copy.23 = bf16[1024,640]{1,0:T(8,128)(2,1)} copy(bf16[1024,640]{1,0:T(8,128)(2,1)S(1)} %bitcast.8) | data formatting | bytes 2621440
  (10 shorter events, 0.1 us)
Async XLA Ops:
  0.6 13.2 %copy-start.1 = (f32[640]{0:T(1024)S(1)}, f32[640]{0:T(1024)}, u32[]{:S(2)}) copy-start(f32[640]{0:T(1024)} %param.24) | copy-start | bytes 7684
  0.7 47.4 %all-to-all-start = ((bf16[64,16,640]{2,1,0:T(8,128)(2,1)}), bf16[64,16,640]{2,1,0:T(8,128)(2,1)}, u32[]{:S(2)}, u32[]{:S(2)}) async-start(bf16[64,16,640]{2,1,0:T(8,128)(2,1)} %bitcast.9), calls=%async_computation | async-start | bytes 2621440 | tf_op jit(solution)/shard_map/all_to_all | solution.py:526
  19.1 2.9 %collective-permute-start = (f32[1,128]{1,0:T(1,128)}, f32[1,128]{1,0:T(1,128)S(1)}, u32[]{:S(2)}, u32[]{:S(2)}) collective-permute-start(f32[1,128]{1,0:T(1,128)} %shard_map.197), channel_id=1, source_target_pairs={{0,1},{1,0},{2,3},{3,2},{4,5},{5,4},{6,7},{7,6},{8,9},{9,8},{10,11... | collective-permute-start | bytes 1544 | tf_op jit(solution)/shard_map/ppermute | solution.py:365
  22.7 4.3 %collective-permute-start.1 = (f32[1,128]{1,0:T(1,128)S(1)}, f32[1,128]{1,0:T(1,128)S(1)}, u32[]{:S(2)}, u32[]{:S(2)}) collective-permute-start(f32[1,128]{1,0:T(1,128)S(1)} %add.6), channel_id=1, source_target_pairs={{0,2},{1,3},{2,0},{3,1},{4,6},{5,7},{6,4},{7,5},{8,10},{9,11},{10,... | collective-permute-start | bytes 1544 | tf_op jit(solution)/shard_map/ppermute | solution.py:365
  27.0 2.8 %collective-permute-start.2 = (f32[1,128]{1,0:T(1,128)S(1)}, f32[1,128]{1,0:T(1,128)S(1)}, u32[]{:S(2)}, u32[]{:S(2)}) collective-permute-start(f32[1,128]{1,0:T(1,128)S(1)} %add.7), channel_id=1, source_target_pairs={{4,0},{0,4},{12,8},{8,12},{20,16},{16,20},{28,24},{24,28},{36,32},... | collective-permute-start | bytes 1544 | tf_op jit(solution)/shard_map/ppermute | solution.py:381
  29.8 13.7 %collective-permute-start.6 = (f32[2,128]{1,0:T(2,128)S(1)}, f32[2,128]{1,0:T(2,128)S(1)}, u32[]{:S(2)}, u32[]{:S(2)}) collective-permute-start(f32[2,128]{1,0:T(2,128)S(1)} %pad_maximum_fusion.1), channel_id=1, source_target_pairs={{32,0},{60,4},{40,8},{4,12},{48,16},{12,20},{56,24},{20,28},{0,32}... | collective-permute-start | bytes 3080 | tf_op jit(solution)/shard_map/ppermute | solution.py:381
  31.0 13.9 %collective-permute-start.5 = (f32[2,128]{1,0:T(2,128)S(1)}, f32[2,128]{1,0:T(2,128)S(1)}, u32[]{:S(2)}, u32[]{:S(2)}) collective-permute-start(f32[2,128]{1,0:T(2,128)S(1)} %pad_maximum_fusion.1), channel_id=1, source_target_pairs={{24,0},{52,4},{32,8},{60,12},{40,16},{4,20},{48,24},{12,28},{56,32... | collective-permute-start | bytes 3080 | tf_op jit(solution)/shard_map/ppermute | solution.py:381
  33.1 11.9 %collective-permute-start.4 = (f32[2,128]{1,0:T(2,128)S(1)}, f32[2,128]{1,0:T(2,128)S(1)}, u32[]{:S(2)}, u32[]{:S(2)}) collective-permute-start(f32[2,128]{1,0:T(2,128)S(1)} %pad_maximum_fusion.1), channel_id=1, source_target_pairs={{16,0},{44,4},{24,8},{52,12},{32,16},{60,20},{40,24},{4,28},{48,32... | collective-permute-start | bytes 3080 | tf_op jit(solution)/shard_map/ppermute | solution.py:381
  35.5 12.3 %collective-permute-start.3 = (f32[2,128]{1,0:T(2,128)S(1)}, f32[2,128]{1,0:T(2,128)S(1)}, u32[]{:S(2)}, u32[]{:S(2)}) collective-permute-start(f32[2,128]{1,0:T(2,128)S(1)} %pad_maximum_fusion.1), channel_id=1, source_target_pairs={{8,0},{36,4},{16,8},{44,12},{24,16},{52,20},{32,24},{60,28},{40,32... | collective-permute-start | bytes 3080 | tf_op jit(solution)/shard_map/ppermute | solution.py:381
  48.0 40.3 %all-to-all-start.1 = ((bf16[64,16,640]{2,1,0:T(8,128)(2,1)}), bf16[64,16,640]{2,1,0:T(8,128)(2,1)S(1)}, u32[]{:S(2)}, u32[]{:S(2)}) async-start(bf16[64,16,640]{2,1,0:T(8,128)(2,1)} %bitcast.10), calls=%async_computation.1 | async-start | bytes 2621440 | tf_op jit(solution)/shard_map/all_to_all | solution.py:537
  54.2 1.4 %collective-permute-start.7 = (f32[8,128]{1,0:T(8,128)S(1)}, f32[8,128]{1,0:T(8,128)S(1)}, u32[]{:S(2)}, u32[]{:S(2)}) collective-permute-start(f32[8,128]{1,0:T(8,128)S(1)} %pad_maximum_fusion), channel_id=1, source_target_pairs={{4,0},{0,4},{12,8},{8,12},{20,16},{16,20},{28,24},{24,28},{36,32},... | collective-permute-start | bytes 12296 | tf_op jit(solution)/shard_map/ppermute | solution.py:381
  55.6 4.6 %collective-permute-start.8 = (f32[24,128]{1,0:T(8,128)S(1)}, f32[24,128]{1,0:T(8,128)S(1)}, u32[]{:S(2)}, u32[]{:S(2)}) collective-permute-start(f32[24,128]{1,0:T(8,128)S(1)} %concatenate.17), channel_id=1, source_target_pairs={{128,0},{132,4},{136,8},{140,12},{144,16},{148,20},{152,24},{156,2... | collective-permute-start | bytes 36872 | tf_op jit(solution)/shard_map/ppermute | solution.py:381
  60.2 3.9 %copy-start = (f32[48,128]{1,0:T(8,128)}, f32[48,128]{1,0:T(8,128)S(1)}, u32[]{:S(2)}) copy-start(f32[48,128]{1,0:T(8,128)S(1)} %concatenate.18.near_ref) | copy-start | bytes 73732
  60.2 3.9 %collective-permute-start.9 = (f32[48,128]{1,0:T(8,128)S(1)}, f32[48,128]{1,0:T(8,128)S(1)}, u32[]{:S(2)}, u32[]{:S(2)}) collective-permute-start(f32[48,128]{1,0:T(8,128)S(1)} %concatenate.18.near_ref), channel_id=1, source_target_pairs={{64,0},{68,4},{72,8},{76,12},{80,16},{84,20},{88,24},{92,28},{96,3... | collective-permute-start | bytes 73736 | tf_op jit(solution)/shard_map/ppermute | solution.py:381
  64.1 0.6 copy-start.2
